TPU v7x, 32 devices: a whole 2x2x4 slice. The times are simulated.
32 devices in a mesh: seq: 4 (over z), fsdp: 8 (over y, x, core).
Axes of the slice: x: 2, y: 2, z: 4, core: 2. Of those that a mesh axis runs over, the one named last changes fastest.
Arguments:
- inputs: bfloat16 [2, 8192, 1024], P(None, ('seq', 'fsdp')), may hold values from -6 to 6
- cotangent: bfloat16 [2, 8192, 1024], P(None, ('seq', 'fsdp')), may hold values from -6 to 6
- segment_ids: int32 [2, 8192], replicated, may hold values from 0 to 3, as said below
- norm1_gain: bfloat16 [1024], P('fsdp'), may hold values from 0.099609375 to 1.8984375
- norm1_bias: bfloat16 [1024], P('fsdp'), may hold values from -3 to 3
- qkv_weight: bfloat16 [1024, 3072], P(None, 'fsdp'), may hold values from -0.1875 to 0.1875
- qv_bias: bfloat16 [16, 128], P('fsdp'), may hold values from -3 to 3
- out_weight: bfloat16 [1024, 1024], P('fsdp'), may hold values from -1.5 to 1.5
- out_bias: bfloat16 [1024], P('fsdp'), may hold values from -3 to 3
- norm2_gain: bfloat16 [1024], P('fsdp'), may hold values from 0.099609375 to 1.8984375
- norm2_bias: bfloat16 [1024], P('fsdp'), may hold values from -3 to 3
- fc_weight: bfloat16 [1024, 4096], P(None, 'fsdp'), may hold values from -0.1875 to 0.1875
- fc_bias: bfloat16 [4096], P('fsdp'), may hold values from -3 to 3
- proj_weight: bfloat16 [4096, 1024], P('fsdp'), may hold values from -0.09375 to 0.09375
- proj_bias: bfloat16 [1024], P('fsdp'), may hold values from -3 to 3
Outputs:
- layer_output: bfloat16 [2, 8192, 1024], P(None, ('seq', 'fsdp'))
- input_grad: bfloat16 [2, 8192, 1024], P(None, ('seq', 'fsdp'))
- norm1_gain_grad: float32 [1024], P('fsdp')
- norm1_bias_grad: float32 [1024], P('fsdp')
- qkv_weight_grad: float32 [1024, 3072], P(None, 'fsdp')
- qv_bias_grad: float32 [16, 128], P('fsdp')
- out_weight_grad: float32 [1024, 1024], P('fsdp')
- out_bias_grad: float32 [1024], P('fsdp')
- norm2_gain_grad: float32 [1024], P('fsdp')
- norm2_bias_grad: float32 [1024], P('fsdp')
- fc_weight_grad: float32 [1024, 4096], P(None, 'fsdp')
- fc_bias_grad: float32 [4096], P('fsdp')
- proj_weight_grad: float32 [4096, 1024], P('fsdp')
- proj_bias_grad: float32 [1024], P('fsdp')
Inputs may be any that keep to these rules, and one draw needn't show every extreme that they name: `segment_ids`: along each sequence the ids start at 0 and never fall, rising by at most one from a token to the next. In every draw one sequence, chosen by the seed, is a single document; every other sequence holds exactly 4 documents.
All inputs are finite; a program needn't handle non-finite values.
Results may differ from a plain program's by a relative error of at most 0.012.
The roundings to bfloat16 on the way count: a program that leaves them out, or rounds other values in their place, can miss the bound.
Values may be sent and summed in bfloat16 or wider, within the bound.
A program may use at most 256 MiB of HBM per device.

v0:
```python
import math

import jax
import jax.numpy as jnp
from jax import lax
from jax.sharding import PartitionSpec as P

H = 16
HD = 64
WINDOW = 1024


norm_eps = 1e-05
neg_fill = -1e30


def from_behind(block, axis, distance):
    devices = range(lax.axis_size(axis))
    route = [(i - distance, i) for i in devices if i - distance in devices]
    return lax.ppermute(block, axis, route)


def layer_norm(values, gain, offset):
    centre = values - jnp.mean(values, axis=-1, keepdims=True)
    spread = jnp.mean(centre * centre, axis=-1, keepdims=True)
    return centre * lax.rsqrt(spread + norm_eps) * gain + offset


def gelu_tanh(values):
    return jax.nn.gelu(values, approximate=True)


def full_bias(bias_rows):
    head_size = bias_rows.shape[1] // 2
    query_part = bias_rows[:, :head_size]
    stacked = jnp.stack([query_part, jnp.zeros_like(query_part), bias_rows[:, head_size:]], axis=1)
    return stacked.reshape(-1)


def affine(operand, weight, offset):
    return jnp.einsum("sre,ef->srf", operand, weight, preferred_element_type=jnp.float32) + offset


def bias_grads(grad_rows, head_size):
    summed = jnp.sum(grad_rows, axis=(0, 1), dtype=jnp.float32).reshape(-1, 3, head_size)
    return jnp.concatenate([summed[:, 0], summed[:, 2]], axis=-1)


def block_scores(queries, key_rows, segment_ext, block_start, qblock, window, score_scale):
    query_block = lax.dynamic_slice_in_dim(queries, block_start, qblock, 2)
    key_block = lax.dynamic_slice_in_dim(key_rows, block_start, window + qblock, 2)
    query_ids = lax.dynamic_slice_in_dim(segment_ext, block_start + window, qblock, 1)
    key_ids = lax.dynamic_slice_in_dim(segment_ext, block_start, window + qblock, 1)
    row_pos = lax.broadcasted_iota(jnp.int32, (qblock, window + qblock), 0)
    col_pos = lax.broadcasted_iota(jnp.int32, (qblock, window + qblock), 1)
    in_window = (col_pos > row_pos) & (col_pos <= row_pos + window)
    allowed = in_window[None, None] & (query_ids[:, None, :, None] == key_ids[:, None, None, :])
    scores = (
        jnp.einsum("shqd,shkd->shqk", query_block, key_block, preferred_element_type=jnp.float32)
        * score_scale
    )
    return (jnp.where(allowed, scores, neg_fill), allowed, query_block, key_block)


def forward(inputs, segment_ids, shards):
    (
        norm1_gain,
        norm1_bias,
        qkv_weight,
        qv_bias,
        out_weight,
        out_bias,
        norm2_gain,
        norm2_bias,
        fc_weight,
        fc_bias,
        proj_weight,
        proj_bias,
    ) = shards
    group_size = lax.axis_size("fsdp")
    seq_index = lax.axis_index("seq")
    seq_count, row_count, _ = inputs.shape
    part_rows = row_count * group_size
    heads_dev = H // group_size
    head_size = HD
    window = WINDOW
    qblock = min(512, part_rows)
    block_count = part_rows // qblock
    score_scale = 1.0 / math.sqrt(head_size)
    (
        out_all,
        fc_all,
        proj_all,
        gain_one,
        offset_one,
        out_offset,
        gain_two,
        offset_two,
        fc_offset,
        proj_offset,
    ) = (
        lax.all_gather(out_weight, "fsdp", axis=0, tiled=True),
        lax.all_gather(fc_weight, "fsdp", axis=1, tiled=True),
        lax.all_gather(proj_weight, "fsdp", axis=0, tiled=True),
        lax.all_gather(norm1_gain, "fsdp", axis=0, tiled=True),
        lax.all_gather(norm1_bias, "fsdp", axis=0, tiled=True),
        lax.all_gather(out_bias, "fsdp", axis=0, tiled=True),
        lax.all_gather(norm2_gain, "fsdp", axis=0, tiled=True),
        lax.all_gather(norm2_bias, "fsdp", axis=0, tiled=True),
        lax.all_gather(fc_bias, "fsdp", axis=0, tiled=True),
        lax.all_gather(proj_bias, "fsdp", axis=0, tiled=True),
    )
    input_float = inputs.astype(jnp.float32)
    normed = layer_norm(input_float, gain_one, offset_one).astype(jnp.bfloat16)
    qkv_all, qv_all = (
        lax.all_gather(qkv_weight, "fsdp", axis=1, tiled=True),
        lax.all_gather(qv_bias, "fsdp", axis=0, tiled=True),
    )
    projected = affine(normed, qkv_all, full_bias(qv_all)).astype(jnp.bfloat16)
    local_qkv = lax.all_to_all(projected, "fsdp", split_axis=2, concat_axis=1, tiled=True)
    shaped = local_qkv.reshape(seq_count, part_rows, heads_dev, 3, head_size)
    queries = jnp.transpose(shaped[:, :, :, 0], (0, 2, 1, 3))
    key_tail = shaped[:, part_rows - window :, :, 1:].reshape(
        seq_count, window, heads_dev * 2 * head_size
    )
    key_prev = from_behind(key_tail, "seq", 1).reshape(seq_count, window, heads_dev, 2, head_size)
    pair_ext = jnp.concatenate([key_prev, shaped[:, :, :, 1:]], axis=1)
    key_rows = jnp.transpose(pair_ext[:, :, :, 0], (0, 2, 1, 3))
    value_rows = jnp.transpose(pair_ext[:, :, :, 1], (0, 2, 1, 3))
    padded_ids = jnp.concatenate(
        [jnp.full((seq_count, window), -1, jnp.int32), segment_ids], axis=1
    )
    segment_ext = lax.dynamic_slice_in_dim(padded_ids, seq_index * part_rows, window + part_rows, 1)

    def attend(block_start):
        scores, allowed, query_block, key_block = block_scores(
            queries, key_rows, segment_ext, block_start, qblock, window, score_scale
        )
        value_block = lax.dynamic_slice_in_dim(value_rows, block_start, window + qblock, 2)
        row_peak = jnp.max(scores, axis=-1, keepdims=True)
        exponent = jnp.exp(scores - row_peak)
        row_total = jnp.sum(exponent, axis=-1, keepdims=True)
        weights_low = (exponent / row_total).astype(jnp.bfloat16)
        attended = jnp.einsum(
            "shqk,shkd->shqd", weights_low, value_block, preferred_element_type=jnp.float32
        )
        return (attended.astype(jnp.bfloat16), row_peak + jnp.log(row_total))

    block_starts = jnp.arange(block_count, dtype=jnp.int32) * qblock
    attended, log_totals = lax.map(attend, block_starts)
    head_out = jnp.transpose(attended, (1, 0, 3, 2, 4)).reshape(
        seq_count, part_rows, heads_dev * head_size
    )
    merged = lax.all_to_all(head_out, "fsdp", split_axis=1, concat_axis=2, tiled=True)
    residual = input_float + affine(merged, out_all, out_offset)
    normed2 = layer_norm(residual, gain_two, offset_two).astype(jnp.bfloat16)
    hidden = affine(normed2, fc_all, fc_offset)
    active = gelu_tanh(hidden).astype(jnp.bfloat16)
    result = (residual + affine(active, proj_all, proj_offset)).astype(jnp.bfloat16)
    stored = dict(
        input_float=input_float,
        normed=normed,
        token_block=normed,
        qkv_all=qkv_all,
        queries=queries,
        key_rows=key_rows,
        value_rows=value_rows,
        segment_ext=segment_ext,
        log_totals=log_totals,
        block_starts=block_starts,
        merged=merged,
        residual=residual,
        normed2=normed2,
        hidden=hidden,
        active=active,
        out_all=out_all,
        fc_all=fc_all,
        proj_all=proj_all,
        gain_one=gain_one,
        offset_one=offset_one,
        gain_two=gain_two,
        offset_two=offset_two,
    )
    return (result, stored)


def norm_backward(values, gain, offset, grad_normed):
    _, norm_back = jax.vjp(layer_norm, values, gain.astype(jnp.float32), offset.astype(jnp.float32))
    return norm_back(grad_normed)


def backward(cotangent, stored):
    queries = stored["queries"]
    key_rows = stored["key_rows"]
    value_rows = stored["value_rows"]
    segment_ext = stored["segment_ext"]
    seq_count, heads_dev, part_rows, head_size = queries.shape
    window = WINDOW
    qblock = min(512, part_rows)
    score_scale = 1.0 / math.sqrt(head_size)
    grad_float = cotangent.astype(jnp.float32)
    proj_bias_part = jnp.sum(cotangent, axis=(0, 1), dtype=jnp.float32)
    proj_weight_part = jnp.einsum(
        "srf,srd->fd", stored["active"], cotangent, preferred_element_type=jnp.float32
    )
    grad_active = jnp.einsum(
        "srd,fd->srf", cotangent, stored["proj_all"], preferred_element_type=jnp.float32
    )
    _, gelu_back = jax.vjp(gelu_tanh, stored["hidden"])
    grad_hidden = gelu_back(grad_active)[0].astype(jnp.bfloat16)
    fc_bias_part = jnp.sum(grad_hidden, axis=(0, 1), dtype=jnp.float32)
    fc_weight_part = jnp.einsum(
        "sre,srf->ef", stored["normed2"], grad_hidden, preferred_element_type=jnp.float32
    )
    grad_normed2 = jnp.einsum(
        "srf,ef->sre", grad_hidden, stored["fc_all"], preferred_element_type=jnp.float32
    )
    resid_part, gain_two_part, offset_two_part = norm_backward(
        stored["residual"], stored["gain_two"], stored["offset_two"], grad_normed2
    )
    (
        fc_weight_grad,
        proj_weight_grad,
        gain_two_grad,
        offset_two_grad,
        fc_bias_grad,
        proj_bias_grad,
    ) = (
        lax.psum_scatter(fc_weight_part, "fsdp", scatter_dimension=1, tiled=True),
        lax.psum_scatter(proj_weight_part, "fsdp", scatter_dimension=0, tiled=True),
        lax.psum_scatter(gain_two_part, "fsdp", scatter_dimension=0, tiled=True),
        lax.psum_scatter(offset_two_part, "fsdp", scatter_dimension=0, tiled=True),
        lax.psum_scatter(fc_bias_part, "fsdp", scatter_dimension=0, tiled=True),
        lax.psum_scatter(proj_bias_part, "fsdp", scatter_dimension=0, tiled=True),
    )
    grad_residual = grad_float + resid_part
    grad_attn = grad_residual.astype(jnp.bfloat16)
    out_bias_part = jnp.sum(grad_attn, axis=(0, 1), dtype=jnp.float32)
    out_weight_part = jnp.einsum(
        "sre,srd->ed", stored["merged"], grad_attn, preferred_element_type=jnp.float32
    )
    grad_merged = jnp.einsum(
        "srd,ed->sre", grad_attn, stored["out_all"], preferred_element_type=jnp.float32
    ).astype(jnp.bfloat16)
    grad_heads = lax.all_to_all(grad_merged, "fsdp", split_axis=2, concat_axis=1, tiled=True)
    grad_heads = jnp.transpose(
        grad_heads.reshape(seq_count, part_rows, heads_dev, head_size), (0, 2, 1, 3)
    )

    def attend_back(running, scan_entry):
        block_start, log_total = scan_entry
        key_grads, value_grads = running
        scores, allowed, query_block, key_block = block_scores(
            queries, key_rows, segment_ext, block_start, qblock, window, score_scale
        )
        value_block = lax.dynamic_slice_in_dim(value_rows, block_start, window + qblock, 2)
        grad_block = lax.dynamic_slice_in_dim(grad_heads, block_start, qblock, 2)
        weights_full = jnp.where(allowed, jnp.exp(scores - log_total), 0.0)
        weights_low = weights_full.astype(jnp.bfloat16)
        value_terms = jnp.einsum(
            "shqk,shqd->shkd", weights_low, grad_block, preferred_element_type=jnp.float32
        )
        weight_grads = jnp.einsum(
            "shqd,shkd->shqk", grad_block, value_block, preferred_element_type=jnp.float32
        )
        centred = weight_grads - jnp.sum(weights_full * weight_grads, axis=-1, keepdims=True)
        score_grads = (weights_full * centred).astype(jnp.bfloat16)
        query_grads = (
            jnp.einsum(
                "shqk,shkd->shqd", score_grads, key_block, preferred_element_type=jnp.float32
            )
            * score_scale
        )
        key_terms = (
            jnp.einsum(
                "shqk,shqd->shkd", score_grads, query_block, preferred_element_type=jnp.float32
            )
            * score_scale
        )
        key_grads = lax.dynamic_update_slice_in_dim(
            key_grads,
            lax.dynamic_slice_in_dim(key_grads, block_start, window + qblock, 2) + key_terms,
            block_start,
            2,
        )
        value_grads = lax.dynamic_update_slice_in_dim(
            value_grads,
            lax.dynamic_slice_in_dim(value_grads, block_start, window + qblock, 2) + value_terms,
            block_start,
            2,
        )
        return ((key_grads, value_grads), query_grads)

    ext_zeros = jnp.zeros((seq_count, heads_dev, window + part_rows, head_size), jnp.float32)
    (key_grads, value_grads), query_grads = lax.scan(
        attend_back, (ext_zeros, ext_zeros), (stored["block_starts"], stored["log_totals"])
    )
    query_grads = jnp.transpose(query_grads, (1, 2, 0, 3, 4)).reshape(
        seq_count, heads_dev, part_rows, head_size
    )
    edge_grads = jnp.concatenate([key_grads[:, :, :window], value_grads[:, :, :window]], axis=-1)
    edge_back = from_behind(edge_grads, "seq", -1)
    edge_pad = jnp.pad(edge_back, ((0, 0), (0, 0), (part_rows - window, 0), (0, 0)))
    key_own = key_grads[:, :, window:] + edge_pad[..., :head_size]
    value_own = value_grads[:, :, window:] + edge_pad[..., head_size:]
    grad_local = jnp.stack([query_grads, key_own, value_own], axis=3).astype(jnp.bfloat16)
    grad_local = jnp.transpose(grad_local, (0, 2, 1, 3, 4)).reshape(
        seq_count, part_rows, heads_dev * 3 * head_size
    )
    grad_tokens = lax.all_to_all(grad_local, "fsdp", split_axis=1, concat_axis=2, tiled=True)
    qkv_weight_part = jnp.einsum(
        "sre,srf->ef", stored["normed"], grad_tokens, preferred_element_type=jnp.float32
    )
    qv_bias_part = bias_grads(grad_tokens, head_size)
    grad_normed = jnp.einsum(
        "srf,ef->sre", grad_tokens, stored["qkv_all"], preferred_element_type=jnp.float32
    )
    input_part, gain_one_part, offset_one_part = norm_backward(
        stored["input_float"], stored["gain_one"], stored["offset_one"], grad_normed
    )
    (
        qkv_weight_grad,
        qv_bias_grad,
        out_weight_grad,
        gain_one_grad,
        offset_one_grad,
        out_bias_grad,
    ) = (
        lax.psum_scatter(qkv_weight_part, "fsdp", scatter_dimension=1, tiled=True),
        lax.psum_scatter(qv_bias_part, "fsdp", scatter_dimension=0, tiled=True),
        lax.psum_scatter(out_weight_part, "fsdp", scatter_dimension=0, tiled=True),
        lax.psum_scatter(gain_one_part, "fsdp", scatter_dimension=0, tiled=True),
        lax.psum_scatter(offset_one_part, "fsdp", scatter_dimension=0, tiled=True),
        lax.psum_scatter(out_bias_part, "fsdp", scatter_dimension=0, tiled=True),
    )
    input_grad = (grad_residual + input_part).astype(jnp.bfloat16)
    summed = lax.psum(
        (
            gain_one_grad,
            offset_one_grad,
            qkv_weight_grad,
            qv_bias_grad,
            out_weight_grad,
            out_bias_grad,
            gain_two_grad,
            offset_two_grad,
            fc_weight_grad,
            fc_bias_grad,
            proj_weight_grad,
            proj_bias_grad,
        ),
        "seq",
    )
    return (input_grad, summed)


def body(
    inputs,
    cotangent,
    segment_ids,
    norm1_gain,
    norm1_bias,
    qkv_weight,
    qv_bias,
    out_weight,
    out_bias,
    norm2_gain,
    norm2_bias,
    fc_weight,
    fc_bias,
    proj_weight,
    proj_bias,
):
    shards = (
        norm1_gain,
        norm1_bias,
        qkv_weight,
        qv_bias,
        out_weight,
        out_bias,
        norm2_gain,
        norm2_bias,
        fc_weight,
        fc_bias,
        proj_weight,
        proj_bias,
    )
    result, stored = forward(inputs, segment_ids, shards)
    again_inputs, again_ids, again_shards = lax.optimization_barrier((inputs, segment_ids, shards))
    unused_result, stored = forward(again_inputs, again_ids, again_shards)
    input_grad, summed = backward(cotangent, stored)
    return (
        result,
        input_grad,
        summed[0],
        summed[1],
        summed[2],
        summed[3],
        summed[4],
        summed[5],
        summed[6],
        summed[7],
        summed[8],
        summed[9],
        summed[10],
        summed[11],
    )


def solution(mesh):
    return jax.shard_map(
        body,
        mesh=mesh,
        in_specs=(
            P(None, ("seq", "fsdp"), None),
            P(None, ("seq", "fsdp"), None),
            P(),
            P("fsdp"),
            P("fsdp"),
            P(None, "fsdp"),
            P("fsdp", None),
            P("fsdp", None),
            P("fsdp"),
            P("fsdp"),
            P("fsdp"),
            P(None, "fsdp"),
            P("fsdp"),
            P("fsdp", None),
            P("fsdp"),
        ),
        out_specs=(
            P(None, ("seq", "fsdp"), None),
            P(None, ("seq", "fsdp"), None),
            P("fsdp"),
            P("fsdp"),
            P(None, "fsdp"),
            P("fsdp", None),
            P("fsdp", None),
            P("fsdp"),
            P("fsdp"),
            P("fsdp"),
            P(None, "fsdp"),
            P("fsdp"),
            P("fsdp", None),
            P("fsdp"),
        ),
        check_vma=False,
    )
```

profile of v0, /device:TPU:0, one launch (start us, length us, event | category | flops | bytes accessed | tf_op | source)
XLA Modules:
  0.0 1531.5 jit_solution(14830752520307314150)
XLA Ops:
  75.8 55.0 %all_to_all.99 = bf16[2,256,3072]{1,0,2:T(2,128)(2,1)S(1)} all-to-all(bf16[2,256,3072]{1,0,2:T(2,128)(2,1)} %copy.82), channel_id=1, replica_groups=mesh['seq'=4,'fsdp'=8] {'fsdp'}, dimensions={2} | all-to-all | bytes 6291456 | tf_op jit(solution)/shard_map/all_to_all | solution.py:120
  149.2 15.4 %collective-permute-done.1 = bf16[2,1024,256]{1,2,0:T(8,128)(2,1)} collective-permute-done((bf16[2,1024,256]{1,2,0:T(8,128)(2,1)S(1)}, bf16[2,1024,256]{1,2,0:T(8,128)(2,1)}, u32[]{:S(2)}, u32[]{:S(2)}) %collective-permute-start.1) | collective-permute-done | bytes 1048608 | tf_op jit(solution)/shard_map/ppermute | solution.py:20
  168.8 89.0 %while.43 = (s32[]{:T(128)}, bf16[4,2,2,512,64]{3,4,2,1,0:T(8,128)(2,1)}, f32[4,2,2,512,1]{3,2,1,4,0:T(2,128)S(1)}, s32[4]{0:T(128)S(1)}, s32[2,3072]{1,0:T(2,12...) while((s32[]{:T(128)}, ...), condition=%wide.region_13.14_spmd, body=%wide.region_10.13_spmd.sunk | while | flops 848689664 | bytes 47829776 | solution.py:150
  273.1 18.3 %all-gather.11 = bf16[8,1,128]{2,1,0:T(2,128)(2,1)S(1)} all-gather(bf16[1,1,128]{2,1,0:T(2,128)(2,1)S(1)} %bitcast.316), channel_id=1, replica_groups=mesh['seq'=4,'fsdp'=8] {'fsdp'}, dimensions={0}, use_global_device_ids=true | all-gather | bytes 2304 | tf_op jit(solution)/shard_map/all_gather | solution.py:107
  334.5 13.8 convert_reduce_fusion
  364.5 14.7 all-to-all-done.4
  385.3 277.3 %while.44 = (s32[]{:T(128)}, f32[2,2,3072,64]{2,3,1,0:T(8,128)}, f32[2,2,3072,64]{2,3,1,0:T(8,128)}, bf16[4,2,2,512,64]{3,4,2,1,0:T(8,128)(2,1)}, s32[4]{0:T(128...) while((s32[]{:T(128)}, f32[2,2,3072,64]{2,3,1,0:T(8,128)}, ...), condition=%wide.region_20.21_spmd, body=%wide.region_18.20_spmd.sunk | while | flops 2051537408 | bytes 203781072 | solution.py:295
  677.4 36.6 %collective-permute-done.2 = f32[2,2,1024,128]{2,3,1,0:T(8,128)} collective-permute-done((f32[2,2,1024,128]{2,3,1,0:T(8,128)}, f32[2,2,1024,128]{2,3,1,0:T(8,128)}, u32[]{:S(2)}, u32[]{:S(2)}) %collective-permute-start.2) | collective-permute-done | bytes 2097184 | tf_op jit(solution)/shard_map/ppermute | solution.py:20
  723.0 43.6 %all_to_all.100 = bf16[2,2048,384]{2,0,1:T(2,128)(2,1)S(1)} all-to-all(bf16[2,2048,384]{2,0,1:T(2,128)(2,1)} %copy.92), channel_id=1, replica_groups=mesh['seq'=4,'fsdp'=8] {'fsdp'}, dimensions={1} | all-to-all | bytes 6291456 | tf_op jit(solution)/shard_map/all_to_all | solution.py:310
  777.8 16.9 %convolution_bitcast_fusion.1 = f32[1024,4096]{1,0:T(8,128)} fusion(bf16[2,256,4096]{2,1,0:T(8,128)(2,1)} %copy-done.74, f32[2,256,1024]{2,1,0:T(8,128)} %copy-done.13, f32[1024]{0:T(1024)S(1)} %bitcast.302, f32[1024]{0:T(1024)S(1)} %bitcast.298, f32[2,256]{1,0:T(2,128)S(1)} %copy-done.53, f32[2,256]{1,0:T(2,128)S(1)} %copy-done.40), kind=kOutput, calls=%fused_computation.92 | convolution fusion | flops 4297588736 | bytes 23080960 | tf_op jit(solution)/shard_map/sre,srf->ef/dot_general | solution.py:212
  796.0 15.5 %convolution_bitcast_fusion = f32[4096,1024]{1,0:T(8,128)} fusion(bf16[2,256,1024]{2,1,0:T(8,128)(2,1)S(1)} %copy-done.16, f32[2,256,4096]{2,1,0:T(8,128)} %fusion.85, f32[4096]{0:T(1024)S(1)} %bitcast.293), kind=kOutput, calls=%fused_computation.91 | convolution fusion | flops 4315938816 | bytes 26230784 | tf_op jit(solution)/shard_map/srf,srd->fd/dot_general | solution.py:203
  846.7 54.1 %all_to_all.101 = bf16[2,256,3072]{1,0,2:T(2,128)(2,1)S(1)} all-to-all(bf16[2,256,3072]{1,0,2:T(2,128)(2,1)} %copy.75), channel_id=1, replica_groups=mesh['seq'=4,'fsdp'=8] {'fsdp'}, dimensions={2} | all-to-all | bytes 6291456 | tf_op jit(solution)/shard_map/all_to_all | solution.py:120
  920.0 16.4 %collective-permute-done = bf16[2,1024,256]{1,2,0:T(8,128)(2,1)} collective-permute-done((bf16[2,1024,256]{1,2,0:T(8,128)(2,1)S(1)}, bf16[2,1024,256]{1,2,0:T(8,128)(2,1)}, u32[]{:S(2)}, u32[]{:S(2)}) %collective-permute-start) | collective-permute-done | bytes 1048608 | tf_op jit(solution)/shard_map/ppermute | solution.py:20
  940.5 106.9 %while.42 = (s32[]{:T(128)}, bf16[4,2,2,512,64]{3,4,2,1,0:T(8,128)(2,1)}, s32[4]{0:T(128)S(1)}, s32[2,3072]{1,0:T(2,128)S(1)}, bf16[2,2,2048,64]{2,3,1,0:T(8,128...) while((s32[]{:T(128)}, ...), condition=%wide.region_5.6_spmd, body=%wide.region_2.5_spmd.sunk | while | flops 829818880 | bytes 32051972 | solution.py:150
  1024.4 13.1 fusion.238
  1065.4 25.8 %all-gather.3 = bf16[8,1,128]{2,1,0:T(2,128)(2,1)S(1)} all-gather(bf16[1,1,128]{2,1,0:T(2,128)(2,1)S(1)} %bitcast.317), channel_id=1, replica_groups=mesh['seq'=4,'fsdp'=8] {'fsdp'}, dimensions={0}, use_global_device_ids=true | all-gather | bytes 2304 | tf_op jit(solution)/shard_map/all_gather | solution.py:107
  1125.9 21.2 %reduce-scatter.11.cloned.1.call-done = f32[512,1024]{1,0:T(8,128)} async-done(((f32[4096,1024]{1,0:T(8,128)}), f32[512,1024]{1,0:T(8,128)}) %reduce-scatter.11.cloned.1.call-update) | async-done | bytes 2097168 | tf_op jit(solution)/shard_map/reduce_scatter | solution.py:230
  1147.1 29.8 %all-gather.26.cloned.1.call-done = bf16[1024,1024]{1,0:T(8,128)(2,1)} async-done(((bf16[128,1024]{1,0:T(8,128)(2,1)}), bf16[1024,1024]{1,0:T(8,128)(2,1)}) %all-gather.26.cloned.1.call-update) | async-done | bytes 2097168 | tf_op jit(solution)/shard_map/all_gather | solution.py:102
  1181.5 53.4 %all-gather.28.cloned.1.call-done = bf16[1024,4096]{1,0:T(8,128)(2,1)} async-done(((bf16[1024,512]{1,0:T(8,128)(2,1)}), bf16[1024,4096]{1,0:T(8,128)(2,1)}) %all-gather.28.cloned.1.call-update) | async-done | bytes 8388624 | tf_op jit(solution)/shard_map/all_gather | solution.py:103
  1234.9 12.5 fusion.82
  1247.4 43.9 %all-gather.30.cloned.1.call-done = bf16[4096,1024]{1,0:T(8,128)(2,1)} async-done(((bf16[512,1024]{1,0:T(8,128)(2,1)}), bf16[4096,1024]{1,0:T(8,128)(2,1)}) %all-gather.30.cloned.1.call-update) | async-done | bytes 8388624 | tf_op jit(solution)/shard_map/all_gather | solution.py:104
  1313.6 25.6 %all-reduce.11 = (f32[1024]{0:T(1024)S(1)}, f32[1024]{0:T(1024)S(1)}, f32[16,128]{1,0:T(8,128)S(1)}, f32[1024]{0:T(1024)S(1)}, f32[1024]{0:T(1024)S(1)}, /*index...) all-reduce(f32[1024]{0:T(1024)S(1)} %get-tuple-element.378, ...), channel_id=2, replica_groups=mesh['seq'=4,'fsdp'=8] {'fsdp'}, use_global_device_ids=true, to_apply=%region_24.25.clone | all-reduce | flops 12288 | bytes 98304
  1339.7 13.3 all-reduce.12
  1353.1 165.4 %all-reduce.16.cloned.1.call-done = (f32[1024,384]{1,0:T(8,128)}, f32[128,1024]{1,0:T(8,128)}, f32[1024,512]{1,0:T(8,128)}, f32[512,1024]{1,0:T(8,128)}) async-done(((f32[1024,384]{1,0:T(8,128)}, f32[128,1024]{1,0:T(8,128)}, f32[1024,512]{1,0:T(8,128)}, f32[512,1024]{1,0:T(8,128)}), (f32[1024,384]{1,0:T(8,128)}, f32[128,1024]{1,0:T(8,128)}, f32[1024,512]{1,0:T(8,128)}, ...) | async-done | bytes 6291472 | tf_op jit(solution)/shard_map/psum | solution.py:337
  (500 shorter events, 755.3 us)
Async XLA Ops:
  7.2 52.1 %all-gather.34.cloned.1.call-start = ((), (), s32[]{:S(2)}) async-start(), calls=%async_computation.15 | async-start | bytes 7077888 | tf_op jit(solution)/shard_map/all_gather | solution.py:116
  7.9 309.5 %all-gather.36.cloned.1.call-start = ((), (), s32[]{:S(2)}) async-start(), calls=%async_computation.16 | async-start | bytes 2359296 | tf_op jit(solution)/shard_map/all_gather | solution.py:102
  8.7 313.7 %all-gather.38.cloned.1.call-start = ((), (), s32[]{:S(2)}) async-start(), calls=%async_computation.17 | async-start | bytes 9437184 | tf_op jit(solution)/shard_map/all_gather | solution.py:103
  9.4 325.1 %all-gather.32.cloned.1.call-start = ((), (), s32[]{:S(2)}) async-start(), calls=%async_computation.14 | async-start | bytes 9437184 | tf_op jit(solution)/shard_map/all_gather | solution.py:104
  141.6 23.0 %collective-permute-start.1 = (bf16[2,1024,256]{1,2,0:T(8,128)(2,1)S(1)}, bf16[2,1024,256]{1,2,0:T(8,128)(2,1)}, u32[]{:S(2)}, u32[]{:S(2)}) collective-permute-start(bf16[2,1024,256]{1,2,0:T(8,128)(2,1)S(1)} %bitcast.280), channel_id=1, source_target_pairs={{0,8},{8,16},{16,24},{1,9},{9,17},{17,25},{2,10},{10,18},{18,26},{... | collective-permute-start | bytes 3145736 | tf_op jit(solution)/shard_map/ppermute | solution.py:20
  263.7 44.1 %copy-start.56 = (bf16[512]{0:T(512)(128)(2,1)S(1)}, bf16[512]{0:T(512)(128)(2,1)}, u32[]{:S(2)}) copy-start(bf16[512]{0:T(512)(128)(2,1)} %param.33) | copy-start | bytes 3076
  269.5 46.8 %all-to-all-start.3 = ((bf16[2,2048,128]{2,0,1:T(2,128)(2,1)}), bf16[2,2048,128]{2,0,1:T(2,128)(2,1)S(1)}, u32[]{:S(2)}, u32[]{:S(2)}) async-start(bf16[2,2048,128]{2,0,1:T(2,128)(2,1)} %reshape.382), calls=%async_computation.3 | async-start | bytes 2097152 | tf_op jit(solution)/shard_map/all_to_all | solution.py:154
  299.2 54.7 %copy-start.50 = (f32[8,1,128]{2,1,0:T(1,128)}, f32[8,1,128]{2,1,0:T(1,128)S(1)}, u32[]{:S(2)}) copy-start(f32[8,1,128]{2,1,0:T(1,128)S(1)} %convert_element_type.207) | copy-start | bytes 12292
  360.3 18.9 %all-to-all-start.4 = ((bf16[2,256,1024]{1,0,2:T(2,128)(2,1)}), bf16[2,256,1024]{1,0,2:T(2,128)(2,1)S(1)}, u32[]{:S(2)}, u32[]{:S(2)}) async-start(bf16[2,256,1024]{1,0,2:T(2,128)(2,1)} %copy.88), calls=%async_computation.4 | async-start | bytes 2097152 | tf_op jit(solution)/shard_map/all_to_all | solution.py:245
  363.8 466.4 %all-gather.24.cloned.1.call-start = ((), (), s32[]{:S(2)}) async-start(), calls=%async_computation.10 | async-start | bytes 7077888 | tf_op jit(solution)/shard_map/all_gather | solution.py:116
  364.4 761.5 %reduce-scatter.7.cloned.1.call-start = ((), (), s32[]{:S(2)}) async-start(), calls=%async_computation.19 | async-start | bytes 4718592 | tf_op jit(solution)/shard_map/reduce_scatter | solution.py:331
  666.8 47.2 %collective-permute-start.2 = (f32[2,2,1024,128]{2,3,1,0:T(8,128)}, f32[2,2,1024,128]{2,3,1,0:T(8,128)}, u32[]{:S(2)}, u32[]{:S(2)}) collective-permute-start(f32[2,2,1024,128]{2,3,1,0:T(8,128)} %pad_maximum_fusion), channel_id=1, source_target_pairs={{8,0},{16,8},{24,16},{9,1},{17,9},{25,17},{10,2},{18,10},{26,18},{... | collective-permute-start | bytes 6291464 | tf_op jit(solution)/shard_map/ppermute | solution.py:20
  671.6 454.3 %reduce-scatter.5.cloned.1.call-start = ((), (), s32[]{:S(2)}) async-start(), calls=%async_computation.18 | async-start | bytes 14155776 | tf_op jit(solution)/shard_map/reduce_scatter | solution.py:329
  777.1 348.8 %reduce-scatter.9.cloned.1.call-start = ((), (), s32[]{:S(2)}) async-start(), calls=%async_computation.20 | async-start | bytes 18874368 | tf_op jit(solution)/shard_map/reduce_scatter | solution.py:229
  794.7 352.4 %reduce-scatter.11.cloned.1.call-start = ((), (), s32[]{:S(2)}) async-start(), calls=%async_computation.21 | async-start | bytes 18874368 | tf_op jit(solution)/shard_map/reduce_scatter | solution.py:230
  811.5 365.4 %all-gather.26.cloned.1.call-start = ((), (), s32[]{:S(2)}) async-start(), calls=%async_computation.11 | async-start | bytes 2359296 | tf_op jit(solution)/shard_map/all_gather | solution.py:102
  812.1 422.8 %all-gather.28.cloned.1.call-start = ((), (), s32[]{:S(2)}) async-start(), calls=%async_computation.12 | async-start | bytes 9437184 | tf_op jit(solution)/shard_map/all_gather | solution.py:103
  812.8 478.4 %all-gather.30.cloned.1.call-start = ((), (), s32[]{:S(2)}) async-start(), calls=%async_computation.13 | async-start | bytes 9437184 | tf_op jit(solution)/shard_map/all_gather | solution.py:104
  911.9 24.4 %collective-permute-start = (bf16[2,1024,256]{1,2,0:T(8,128)(2,1)S(1)}, bf16[2,1024,256]{1,2,0:T(8,128)(2,1)}, u32[]{:S(2)}, u32[]{:S(2)}) collective-permute-start(bf16[2,1024,256]{1,2,0:T(8,128)(2,1)S(1)} %bitcast.282), channel_id=1, source_target_pairs={{0,8},{8,16},{16,24},{1,9},{9,17},{17,25},{2,10},{10,18},{18,26},{... | collective-permute-start | bytes 3145736 | tf_op jit(solution)/shard_map/ppermute | solution.py:20
  1053.4 47.1 %copy-start.67 = (bf16[128]{0:T(256)(128)(2,1)S(1)}, bf16[128]{0:T(256)(128)(2,1)}, u32[]{:S(2)}) copy-start(bf16[128]{0:T(256)(128)(2,1)} %param.30) | copy-start | bytes 772
  1053.4 54.7 %copy-start.69 = (bf16[128]{0:T(256)(128)(2,1)S(1)}, bf16[128]{0:T(256)(128)(2,1)}, u32[]{:S(2)}) copy-start(bf16[128]{0:T(256)(128)(2,1)} %param.31) | copy-start | bytes 772
  1053.4 63.6 %copy-start.70 = (bf16[128]{0:T(256)(128)(2,1)S(1)}, bf16[128]{0:T(256)(128)(2,1)}, u32[]{:S(2)}) copy-start(bf16[128]{0:T(256)(128)(2,1)} %param.35) | copy-start | bytes 772
  1059.2 65.6 %all-to-all-start.1 = ((bf16[2,2048,128]{2,0,1:T(2,128)(2,1)}), bf16[2,2048,128]{2,0,1:T(2,128)(2,1)S(1)}, u32[]{:S(2)}, u32[]{:S(2)}) async-start(bf16[2,2048,128]{2,0,1:T(2,128)(2,1)} %reshape.381), calls=%async_computation.1 | async-start | bytes 2097152 | tf_op jit(solution)/shard_map/all_to_all | solution.py:154
  1062.8 455.7 %all-reduce.16.cloned.1.call-start = ((), (), s32[]{:S(2)}) async-start(), calls=%async_computation.22 | async-start | bytes 12582912 | tf_op jit(solution)/shard_map/psum | solution.py:337
  (93 other events, 883.7 us)
Sparse Core Ops, SparseCore 0:
  9.9 49.3 all-gather.33
  61.2 37.4 all-gather.35
  100.6 65.5 all-gather.37
  167.9 54.3 all-gather.31
  366.2 49.2 all-gather.23
  671.7 54.5 reduce-scatter.6
  777.2 114.8 reduce-scatter.4
  896.1 119.6 reduce-scatter.8
  1019.8 127.2 reduce-scatter.10
  1149.0 27.8 all-gather.25
  1178.9 55.9 all-gather.27
  1236.8 54.3 all-gather.29
  1294.1 224.3 all-reduce.15
where the time goes:
time: 1540 us; the launch traced here: 1530 us
  waiting for transfers between devices  412 us (27%)
  matrix products  385 us (25%)
  blocking collectives  346 us (22%)
  local copies, waits for them, and re-layouts  211 us (14%)
  other arithmetic  82.6 us (5%)
  loops' own time  55.1 us (4%)
  starting transfers between devices  22.1 us (1%)
  between operations  17 us (1%)
    psum x1, waiting for transfers between devices, backward(): lax.psum((gain_one_grad, offset_one_grad, qkv_weight_grad, qv_bias_grad,...  165 us
    all_to_all x2, blocking collectives, forward(): lax.all_to_all(projected, 'fsdp', split_axis=2, concat_axis=1, tiled=True)  109 us
    ppermute x3, waiting for transfers between devices, from_behind(): return lax.ppermute(block, axis, route)  68.3 us
    dot_general x8, matrix products, block_scores(): jnp.einsum('shqd,shkd->shqk', query_block, key_block, preferred_element_t...  67.6 us
    dot_general x8, matrix products, attend(): jnp.einsum('shqk,shkd->shqd', weights_low, value_block, preferred_element...  58.2 us
    dot_general x7, matrix products, affine(): jnp.einsum('sre,ef->srf', operand, weight, preferred_element_type=jnp.flo...  57.1 us
    all_gather x2, waiting for transfers between devices, forward(): lax.all_gather(fc_weight, 'fsdp', axis=1, tiled=True)  53.4 us
    sub x4, matrix products, attend(): exponent = jnp.exp(scores - row_peak)  45 us
  transfers between devices with their start and end apart: 19, of which 10 were waited for; matrix products, arithmetic and copies ran while one was open for 41% of the time, Pallas kernels for 0%

commit v1 on v0

v1 whole, which is shorter than its diff:
```python
import functools
import jax, jax.numpy as jnp
from jax import lax
from jax.experimental import pallas as pl
from jax.experimental.pallas import tpu as pltpu
from jax.sharding import PartitionSpec as P

HD = 64
WINDOW = 1024
BLK = 256
PENALTY = 1e30


def nt(a, b):
    return lax.dot_general(a, b, (((1,), (1,)), ((), ())), preferred_element_type=jnp.float32)


def nn(a, b):
    return lax.dot_general(a, b, (((1,), (0,)), ((), ())), preferred_element_type=jnp.float32)


def tn(a, b):
    return lax.dot_general(a, b, (((0,), (0,)), ((), ())), preferred_element_type=jnp.float32)


def split3(v):
    hi = v.astype(jnp.bfloat16).astype(jnp.float32)
    rest = v - hi
    mid = rest.astype(jnp.bfloat16).astype(jnp.float32)
    return hi, mid, rest - mid


def merge_edges(mask, tiles):
    return [jnp.where(mask, tiles[0], tiles[-1])] + tiles[1:-1]


def spread_edges(mask, tiles):
    zero = jnp.zeros_like(tiles[0])
    return [jnp.where(mask, tiles[0], zero)] + tiles[1:] + [jnp.where(mask, zero, tiles[0])]


def edge_mask():
    rows = lax.broadcasted_iota(jnp.int32, (BLK, BLK), 0)
    cols = lax.broadcasted_iota(jnp.int32, (BLK, BLK), 1)
    return rows > cols


def fill_keys(heads, qkv_ref, halo_ref, augk_ref, keys, values):
    halo_rows = halo_ref.shape[1]
    rows = qkv_ref.shape[1]
    ones = jnp.ones((1, HD), jnp.bfloat16)
    for h in range(heads):
        c = h * 2 * HD
        for source, base, size in ((halo_ref, 0, halo_rows), (qkv_ref, halo_rows, rows)):
            pair = source[0, :, c : c + 2 * HD]
            keys[h, base : base + size, :] = jnp.concatenate(
                [pair[:, :HD], augk_ref[0, base : base + size, :]], axis=1
            )
            values[h, base : base + size, :] = jnp.concatenate(
                [pair[:, HD:], jnp.broadcast_to(ones, (size, HD))], axis=1
            )


def attend_kernel(heads, qkv_ref, halo_ref, augk_ref, augq_ref, out_ref, q2_ref, keys, values, values_t):
    step = pl.program_id(1)
    nkeys = keys.shape[1]

    @pl.when(step == 0)
    def _():
        fill_keys(heads, qkv_ref, halo_ref, augk_ref, keys, values)
        for h in range(heads):
            for b in range(nkeys // BLK):
                values_t[h, :, b * BLK : (b + 1) * BLK] = values[h, b * BLK : (b + 1) * BLK, :].T

    mask = edge_mask()
    tiles = WINDOW // BLK + 1
    start = pl.multiple_of(step * BLK, BLK)
    lane = lax.broadcasted_iota(jnp.int32, (BLK, 2 * HD), 1)
    lse_lane = augq_ref.shape[2] + HD - 3
    for h in range(heads):
        qc = heads * 2 * HD + h * HD
        q = jnp.concatenate([qkv_ref[0, pl.ds(start, BLK), qc : qc + HD] * 0.125, augq_ref[0]], axis=1)
        scores = [nt(keys[h, pl.ds(start + b * BLK, BLK), :], q) for b in range(tiles)]
        scores = merge_edges(mask, scores)
        peak = functools.reduce(jnp.maximum, scores)
        peak = jnp.max(peak, axis=0, keepdims=True)
        weights = spread_edges(mask, [jnp.exp(s - peak).astype(jnp.bfloat16) for s in scores])
        total = sum(
            nn(values_t[h, :, pl.ds(pl.multiple_of(start + b * BLK, BLK), BLK)], w) for b, w in enumerate(weights)
        )
        sub = lax.broadcasted_iota(jnp.int32, total.shape, 0)
        total = jnp.where(sub == HD + 1, peak, total).T
        norm = total[:, HD : HD + 1]
        out_ref[0, :, h * HD : (h + 1) * HD] = (total[:, :HD] / norm).astype(out_ref.dtype)
        lse = total[:, HD + 1 : HD + 2] + jnp.log(norm)
        hi, mid, low = split3(-lse)
        q2 = q.astype(jnp.float32)
        q2 = jnp.where(lane == lse_lane, hi, q2)
        q2 = jnp.where(lane == lse_lane + 1, mid, q2)
        q2 = jnp.where(lane == lse_lane + 2, low, q2)
        q2_ref[0, h] = q2.astype(jnp.bfloat16)


def attend(qkv, halo, augk, augq, heads):
    seqs, rows, cols = qkv.shape
    ext = augk.shape[1]
    return pl.pallas_call(
        functools.partial(attend_kernel, heads),
        grid=(seqs, rows // BLK),
        in_specs=[
            pl.BlockSpec((1, rows, cols), lambda s, i: (s, 0, 0)),
            pl.BlockSpec((1, WINDOW, heads * 2 * HD), lambda s, i: (s, 0, 0)),
            pl.BlockSpec((1, ext, HD), lambda s, i: (s, 0, 0)),
            pl.BlockSpec((1, BLK, HD), lambda s, i: (s, i, 0)),
        ],
        out_specs=[
            pl.BlockSpec((1, BLK, heads * HD), lambda s, i: (s, i, 0)),
            pl.BlockSpec((1, heads, BLK, 2 * HD), lambda s, i: (s, 0, i, 0)),
        ],
        out_shape=[
            jax.ShapeDtypeStruct((seqs, rows, heads * HD), jnp.bfloat16),
            jax.ShapeDtypeStruct((seqs, heads, rows, 2 * HD), jnp.bfloat16),
        ],
        scratch_shapes=[
            pltpu.VMEM((heads, ext, 2 * HD), jnp.bfloat16),
            pltpu.VMEM((heads, ext, 2 * HD), jnp.bfloat16),
            pltpu.VMEM((heads, 2 * HD, ext), jnp.bfloat16),
        ],
        compiler_params=pltpu.CompilerParams(vmem_limit_bytes=48 * 2**20),
        name="attend",
    )(qkv, halo, augk, augq)


def attend_back_kernel(
    heads, qkv_ref, halo_ref, augk_ref, q2_ref, out_ref, grad_ref, dq_ref, dkv_ref, dhalo_ref,
    keys, values, keys_t, dkeys, dvalues,
):
    step = pl.program_id(1)
    nkeys = keys.shape[1]

    @pl.when(step == 0)
    def _():
        fill_keys(heads, qkv_ref, halo_ref, augk_ref, keys, values)
        for h in range(heads):
            for b in range(nkeys // BLK):
                keys_t[h, :, b * BLK : (b + 1) * BLK] = keys[h, b * BLK : (b + 1) * BLK, :].T
        dkeys[...] = jnp.zeros_like(dkeys)
        dvalues[...] = jnp.zeros_like(dvalues)

    mask = edge_mask()
    tiles = WINDOW // BLK + 1
    start = pl.multiple_of(step * BLK, BLK)
    lane = lax.broadcasted_iota(jnp.int32, (BLK, 2 * HD), 1)
    for h in range(heads):
        q = q2_ref[0, h]
        g = grad_ref[0, :, h * HD : (h + 1) * HD]
        g32 = g.astype(jnp.float32)
        centre = jnp.sum(g32 * out_ref[0, :, h * HD : (h + 1) * HD].astype(jnp.float32), axis=1, keepdims=True)
        hi, mid, low = split3(-centre)
        g2 = jnp.concatenate([g32, jnp.zeros((BLK, HD), jnp.float32)], axis=1)
        g2 = jnp.where(lane == HD, hi, g2)
        g2 = jnp.where(lane == HD + 1, mid, g2)
        g2 = jnp.where(lane == HD + 2, low, g2).astype(jnp.bfloat16)
        spans = [pl.ds(pl.multiple_of(start + b * BLK, BLK), BLK) for b in range(tiles)]
        scores = merge_edges(mask, [nt(keys[h, s, :], q) for s in spans])
        wgrads = merge_edges(mask, [nt(values[h, s, :], g2) for s in spans])
        weights = [jnp.exp(s) for s in scores]
        sgrads = spread_edges(mask, [(w * d).astype(jnp.bfloat16) for w, d in zip(weights, wgrads)])
        weights = spread_edges(mask, [w.astype(jnp.bfloat16) for w in weights])
        for s, w, d in zip(spans, weights, sgrads):
            dvalues[h, s, :] += nn(w, g2)
            dkeys[h, s, :] += nn(d, q)
        dq = sum(nn(keys_t[h, :, s], d) for s, d in zip(spans, sgrads))
        dq_ref[0, :, h * HD : (h + 1) * HD] = (dq.T[:, :HD] * 0.125).astype(dq_ref.dtype)

    @pl.when(step == pl.num_programs(1) - 1)
    def _():
        for h in range(heads):
            c = h * 2 * HD
            dhalo_ref[0, :, c : c + 2 * HD] = jnp.concatenate(
                [dkeys[h, :WINDOW, :HD], dvalues[h, :WINDOW, :HD]], axis=1
            ).astype(dhalo_ref.dtype)
            dkv_ref[0, :, c : c + 2 * HD] = jnp.concatenate(
                [dkeys[h, WINDOW:, :HD], dvalues[h, WINDOW:, :HD]], axis=1
            ).astype(dkv_ref.dtype)


def attend_back(qkv, halo, augk, q2, out, grad, heads):
    seqs, rows, cols = qkv.shape
    ext = augk.shape[1]
    return pl.pallas_call(
        functools.partial(attend_back_kernel, heads),
        grid=(seqs, rows // BLK),
        in_specs=[
            pl.BlockSpec((1, rows, cols), lambda s, i: (s, 0, 0)),
            pl.BlockSpec((1, WINDOW, heads * 2 * HD), lambda s, i: (s, 0, 0)),
            pl.BlockSpec((1, ext, HD), lambda s, i: (s, 0, 0)),
            pl.BlockSpec((1, heads, BLK, 2 * HD), lambda s, i: (s, 0, i, 0)),
            pl.BlockSpec((1, BLK, heads * HD), lambda s, i: (s, i, 0)),
            pl.BlockSpec((1, BLK, heads * HD), lambda s, i: (s, i, 0)),
        ],
        out_specs=[
            pl.BlockSpec((1, BLK, heads * HD), lambda s, i: (s, i, 0)),
            pl.BlockSpec((1, rows, heads * 2 * HD), lambda s, i: (s, 0, 0)),
            pl.BlockSpec((1, WINDOW, heads * 2 * HD), lambda s, i: (s, 0, 0)),
        ],
        out_shape=[
            jax.ShapeDtypeStruct((seqs, rows, heads * HD), jnp.bfloat16),
            jax.ShapeDtypeStruct((seqs, rows, heads * 2 * HD), jnp.float32),
            jax.ShapeDtypeStruct((seqs, WINDOW, heads * 2 * HD), jnp.bfloat16),
        ],
        scratch_shapes=[
            pltpu.VMEM((heads, ext, 2 * HD), jnp.bfloat16),
            pltpu.VMEM((heads, ext, 2 * HD), jnp.bfloat16),
            pltpu.VMEM((heads, 2 * HD, ext), jnp.bfloat16),
            pltpu.VMEM((heads, ext, 2 * HD), jnp.float32),
            pltpu.VMEM((heads, ext, 2 * HD), jnp.float32),
        ],
        compiler_params=pltpu.CompilerParams(vmem_limit_bytes=56 * 2**20),
        name="attend_back",
    )(qkv, halo, augk, q2, out, grad)


def mask_features(segment_ext, docs):
    doc = jnp.arange(docs, dtype=jnp.int32)
    hot = (segment_ext[..., None] == doc).astype(jnp.bfloat16)
    outside = (segment_ext < 0).astype(jnp.bfloat16)[..., None]
    pad = HD - docs - 4
    one = jnp.ones(segment_ext.shape + (3,), jnp.bfloat16)
    zero = jnp.zeros(segment_ext.shape + (pad,), jnp.bfloat16)
    keys = jnp.concatenate([-hot, -outside, zero, one], axis=-1)
    own = hot[:, WINDOW:]
    queries = jnp.concatenate(
        [
            (1 - own) * jnp.bfloat16(PENALTY),
            jnp.full(own.shape[:2] + (1,), PENALTY, jnp.bfloat16),
            jnp.zeros(own.shape[:2] + (pad + 3,), jnp.bfloat16),
        ],
        axis=-1,
    )
    return keys, queries


norm_eps = 1e-05


def standardize(values):
    centre = values - jnp.mean(values, axis=-1, keepdims=True)
    spread = jnp.mean(centre * centre, axis=-1, keepdims=True)
    rate = lax.rsqrt(spread + norm_eps)
    return centre * rate, rate


def norm_grad(direction, z, rate):
    mean_d = jnp.mean(direction, axis=-1, keepdims=True)
    mean_dz = jnp.mean(direction * z, axis=-1, keepdims=True)
    return rate * (direction - mean_d - z * mean_dz)


def from_behind(block, axis, distance):
    devices = range(lax.axis_size(axis))
    route = [(i - distance, i) for i in devices if i - distance in devices]
    return lax.ppermute(block, axis, route)


def pack_columns(array, heads):
    parts = array.reshape(array.shape[:-1] + (heads, 3 * HD))
    lead = array.shape[:-1]
    return jnp.concatenate(
        [parts[..., HD:].reshape(lead + (-1,)), parts[..., :HD].reshape(lead + (-1,))], axis=-1
    )


def unpack_columns(array, heads):
    lead = array.shape[:-1]
    pairs = array[..., : heads * 2 * HD].reshape(lead + (heads, 2 * HD))
    queries = array[..., heads * 2 * HD :].reshape(lead + (heads, HD))
    return jnp.concatenate([queries, pairs], axis=-1).reshape(lead + (-1,))


def dot(subscripts, a, b):
    return jnp.einsum(subscripts, a, b, preferred_element_type=jnp.float32)


def body(
    inputs, cotangent, segment_ids, norm1_gain, norm1_bias, qkv_weight, qv_bias, out_weight, out_bias,
    norm2_gain, norm2_bias, fc_weight, fc_bias, proj_weight, proj_bias,
):
    group = lax.axis_size("fsdp")
    seqs, local_rows, width = inputs.shape
    part_rows = local_rows * group
    heads = qkv_weight.shape[1] // (3 * HD)
    docs = segment_ids.shape[1] // (2 * WINDOW)
    seq_index = lax.axis_index("seq")
    shard = norm1_gain.shape[0]

    small = jnp.concatenate([norm1_gain, norm1_bias, out_bias, norm2_gain, norm2_bias, proj_bias, fc_bias])
    small = lax.all_gather(small, "fsdp")
    gain1, offset1, out_off, gain2, offset2, proj_off = (
        small[:, i * shard : (i + 1) * shard].reshape(-1).astype(jnp.float32) for i in range(6)
    )
    fc_off = small[:, 6 * shard :].reshape(-1).astype(jnp.float32)
    out_all = lax.all_gather(out_weight, "fsdp", axis=0, tiled=True)
    fc_all = lax.all_gather(fc_weight, "fsdp")
    proj_all = lax.all_gather(proj_weight, "fsdp")

    padded_ids = jnp.concatenate([jnp.full((seqs, WINDOW), -1, jnp.int32), segment_ids], axis=1)
    segment_ext = lax.dynamic_slice_in_dim(padded_ids, seq_index * part_rows, WINDOW + part_rows, 1)
    augk, augq = mask_features(segment_ext, docs)

    x = inputs.astype(jnp.float32)
    z1, rate1 = standardize(x)
    normed1 = (z1 * gain1 + offset1).astype(jnp.bfloat16)
    normed1 = lax.all_gather(normed1, "fsdp", axis=1, tiled=True)
    packed_weight = pack_columns(qkv_weight, heads)
    head_bias = qv_bias.astype(jnp.float32)
    head_bias = jnp.concatenate(
        [head_bias[:, :HD], jnp.zeros((heads, HD), jnp.float32), head_bias[:, HD:]], axis=1
    ).reshape(-1)
    packed_bias = pack_columns(head_bias, heads)
    qkv = (dot("sre,ef->srf", normed1, packed_weight) + packed_bias).astype(jnp.bfloat16)
    halo = from_behind(qkv[:, part_rows - WINDOW :, : heads * 2 * HD], "seq", 1)
    head_out, q2 = attend(qkv, halo, augk, augq, heads)
    merged = lax.all_to_all(head_out, "fsdp", split_axis=1, concat_axis=2, tiled=True)
    resid = x + dot("sre,ef->srf", merged, out_all) + out_off
    z2, rate2 = standardize(resid)
    normed2 = (z2 * gain2 + offset2).astype(jnp.bfloat16)
    fc_offset = fc_off.reshape(group, -1)
    hidden = dot("sre,gef->gsrf", normed2, fc_all) + fc_offset[:, None, None]
    active, gelu_back = jax.vjp(lambda v: jax.nn.gelu(v, approximate=True), hidden)
    active = active.astype(jnp.bfloat16)
    layer_output = (resid + dot("gsrf,gfd->srd", active, proj_all) + proj_off).astype(jnp.bfloat16)

    cot32 = cotangent.astype(jnp.float32)
    proj_bias_part = jnp.sum(cot32, axis=(0, 1))
    proj_weight_part = dot("gsrf,srd->gfd", active, cotangent)
    g_hidden = gelu_back(dot("srd,gfd->gsrf", cotangent, proj_all))[0].astype(jnp.bfloat16)
    fc_bias_part = jnp.sum(g_hidden, axis=(1, 2), dtype=jnp.float32).reshape(-1)
    fc_weight_part = dot("sre,gsrf->gef", normed2, g_hidden)
    g_norm2 = dot("gsrf,gef->sre", g_hidden, fc_all)
    gain2_part = jnp.sum(g_norm2 * z2, axis=(0, 1))
    offset2_part = jnp.sum(g_norm2, axis=(0, 1))
    g_resid = cot32 + norm_grad(g_norm2 * gain2, z2, rate2)
    g_attn = g_resid.astype(jnp.bfloat16)
    out_bias_part = jnp.sum(g_attn, axis=(0, 1), dtype=jnp.float32)
    out_weight_part = dot("sre,srd->ed", merged, g_attn)
    g_merged = dot("srd,ed->sre", g_attn, out_all).astype(jnp.bfloat16)
    g_heads = lax.all_to_all(g_merged, "fsdp", split_axis=2, concat_axis=1, tiled=True)

    low = jnp.bfloat16
    fc_grad = lax.psum_scatter(fc_weight_part.astype(low), "fsdp")
    proj_grad = lax.psum_scatter(proj_weight_part.astype(low), "fsdp")
    out_grad = lax.psum_scatter(out_weight_part.astype(low), "fsdp", scatter_dimension=0, tiled=True)
    fc_grad, proj_grad, out_grad = lax.psum((fc_grad, proj_grad, out_grad), "seq")

    dq, dkv, dhalo = attend_back(qkv, halo, augk, q2, head_out, g_heads, heads)
    edge = from_behind(dhalo, "seq", -1)
    edge = jnp.pad(edge.astype(jnp.float32), ((0, 0), (part_rows - WINDOW, 0), (0, 0)))
    g_qkv = jnp.concatenate([(dkv + edge).astype(jnp.bfloat16), dq], axis=-1)
    qkv_grad = dot("sre,srf->ef", normed1, g_qkv)
    qkv_colsum = jnp.sum(g_qkv, axis=(0, 1), dtype=jnp.float32)
    g_norm1 = dot("srf,ef->sre", g_qkv, packed_weight).astype(jnp.bfloat16)
    g_norm1 = lax.psum_scatter(g_norm1, "fsdp", scatter_dimension=1, tiled=True).astype(jnp.float32)
    gain1_part = jnp.sum(g_norm1 * z1, axis=(0, 1))
    offset1_part = jnp.sum(g_norm1, axis=(0, 1))
    input_grad = (g_resid + norm_grad(g_norm1 * gain1, z1, rate1)).astype(jnp.bfloat16)

    qkv_grad = lax.psum(qkv_grad.astype(low), "seq").astype(jnp.float32)
    qkv_grad = unpack_columns(qkv_grad, heads)
    col = unpack_columns(qkv_colsum, heads).reshape(heads, 3 * HD)
    col = lax.psum(jnp.concatenate([col[:, :HD], col[:, 2 * HD :]], axis=1), "seq")
    vectors = jnp.concatenate(
        [
            v.reshape(group, -1)
            for v in (gain1_part, offset1_part, out_bias_part, gain2_part, offset2_part, proj_bias_part, fc_bias_part)
        ],
        axis=1,
    )
    vectors = lax.psum_scatter(vectors, "fsdp")
    vectors = lax.psum(vectors, "seq")
    parts = [vectors[i * shard : (i + 1) * shard] for i in range(6)] + [vectors[6 * shard :]]
    f32 = jnp.float32
    return (
        layer_output, input_grad, parts[0], parts[1], qkv_grad, col, out_grad.astype(f32), parts[2], parts[3],
        parts[4], fc_grad.astype(f32), parts[6], proj_grad.astype(f32), parts[5],
    )


def solution(mesh):
    tokens = P(None, ("seq", "fsdp"), None)
    rows, cols, vec = P("fsdp", None), P(None, "fsdp"), P("fsdp")
    return jax.shard_map(
        body,
        mesh=mesh,
        in_specs=(tokens, tokens, P(), vec, vec, cols, rows, rows, vec, vec, vec, cols, vec, rows, vec),
        out_specs=(tokens, tokens, vec, vec, cols, rows, rows, vec, vec, vec, cols, vec, rows, vec),
        check_vma=False,
    )
```

time: 1540 us -> 668 us (0.43)
  matrix products: 385 us -> 99.8 us
  blocking collectives: 346 us -> 69.7 us
  local copies, waits for them, and re-layouts: 211 us -> 38.4 us
  waiting for transfers between devices: 412 us -> 330 us
  Pallas kernels: 0 us -> 74.3 us
  other arithmetic: 82.6 us -> 23.6 us
  loops' own time: 55.1 us -> 0 us
    dot_general x47 -> x12, matrix products: 340 us -> 99.8 us  [dot(): return jnp.einsum(subscripts, a, b, preferred_element_type=jnp.float32)]
    all_gather x15 -> x1, blocking collectives: 154 us -> 10.6 us  [body(): small = lax.all_gather(small, 'fsdp')]
    all_to_all x3 -> x1, blocking collectives: 153 us -> 20.3 us  [body(): lax.all_to_all(g_merged, 'fsdp', split_axis=2, concat_axis=1, tiled=True)]
    reduce_scatter x4, waiting for transfers between devices: 21.2 us -> 111 us  [the longest x1 74.9 us: body(): lax.psum_scatter(g_norm1, 'fsdp', scatter_dimension=1, tiled=True)]
    psum x1, waiting for transfers between devices: 165 us -> 80.1 us  [body(): qkv_grad = lax.psum(qkv_grad.astype(low), 'seq').astype(jnp.float32)]
    dynamic_update_slice x8 -> x0, local copies, waits for them, and re-layouts: 77.3 us -> none  [the longest x4 38.7 us: attend_back(): lax.dynamic_update_slice_in_dim(value_grads, lax.dynamic_slice_in_dim(val...]
    pallas_call x0 -> x2, Pallas kernels: none -> 74.3 us  [the longest x1 41.1 us: attend_back(): pl.pallas_call(functools.partial(attend_back_kernel, heads), grid=(seqs,...]
    all_gather x8 -> x4, waiting for transfers between devices: 139 us -> 76.5 us  [the longest x1 46.2 us: body(): normed1 = lax.all_gather(normed1, 'fsdp', axis=1, tiled=True)]
  transfers between devices with their start and end apart: 19 -> 12, of which waited for: 10 -> 8; matrix products, arithmetic and copies ran while one was open for 41% -> 18% of each run, Pallas kernels for 0% -> 11%
where the time goes in v1:
time: 668 us; the launch traced here: 660 us
  waiting for transfers between devices  330 us (49%)
  matrix products  99.8 us (15%)
  Pallas kernels  74.3 us (11%)
  blocking collectives  69.7 us (10%)
  local copies, waits for them, and re-layouts  38.4 us (6%)
  other arithmetic  23.6 us (4%)
  between operations  14.9 us (2%)
  starting transfers between devices  10.1 us (2%)
    dot_general x12, matrix products, dot(): return jnp.einsum(subscripts, a, b, preferred_element_type=jnp.float32)  99.8 us
    psum x1, waiting for transfers between devices, body(): qkv_grad = lax.psum(qkv_grad.astype(low), 'seq').astype(jnp.float32)  80.1 us
    reduce_scatter x1, waiting for transfers between devices, body(): lax.psum_scatter(g_norm1, 'fsdp', scatter_dimension=1, tiled=True)  74.9 us
    all_gather x1, waiting for transfers between devices, body(): normed1 = lax.all_gather(normed1, 'fsdp', axis=1, tiled=True)  46.2 us
    ppermute x2, waiting for transfers between devices, from_behind(): return lax.ppermute(block, axis, route)  45.4 us
    pallas_call x1, Pallas kernels, attend_back(): pl.pallas_call(functools.partial(attend_back_kernel, heads), grid=(seqs,...  41.1 us
    reduce_scatter x1, waiting for transfers between devices, body(): proj_grad = lax.psum_scatter(proj_weight_part.astype(low), 'fsdp')  35.6 us
    pallas_call x1, Pallas kernels, attend(): pl.pallas_call(functools.partial(attend_kernel, heads), grid=(seqs, rows...  33.3 us
  transfers between devices with their start and end apart: 12, of which 8 were waited for; matrix products, arithmetic and copies ran while one was open for 18% of the time, Pallas kernels for 11%

profile of v1, /device:TPU:0, one launch (start us, length us, event | category | flops | bytes accessed | tf_op | source)
XLA Modules:
  0.0 660.4 jit_solution(14045373559137695829)
XLA Ops:
  13.2 10.6 %all-gather.3 = bf16[8,1,1280]{2,1,0:T(2,128)(2,1)S(1)} all-gather(bf16[1,1,1280]{2,1,0:T(2,128)(2,1)S(1)} %reshape.209), channel_id=2, replica_groups=mesh['seq'=4,'fsdp'=8] {'fsdp'}, dimensions={0}, use_global_device_ids=true | all-gather | bytes 23040 | tf_op jit(solution)/shard_map/all_gather | solution.py:298
  37.0 46.2 %all-gather.9.cloned.1.call-done = bf16[2,2048,1024]{2,1,0:T(8,128)(2,1)} async-done(((bf16[2,256,1024]{2,1,0:T(8,128)(2,1)}), bf16[2,2048,1024]{2,1,0:T(8,128)(2,1)}) %all-gather.9.cloned.1.call-update) | async-done | bytes 8388624 | tf_op jit(solution)/shard_map/all_gather | solution.py:314
  83.2 8.0 %add_convert_fusion.qkv_ref = bf16[2,2048,384]{2,1,0:T(8,128)(2,1)S(1)} fusion(bf16[2,2048,1024]{2,1,0:T(8,128)(2,1)} %all-gather.9.cloned.1.call-done, f32[384]{0:T(512)S(1)} %pad_maximum_fusion.4, bf16[1024,128]{1,0:T(8,128)(2,1)S(1)} %copy.71, bf16[1024,256]{1,0:T(8,128)(2,1)} %copy.95), kind=kOutput, calls=%fused_computation.20 | convolution fusion | flops 3225944064 | bytes 12322304 | tf_op jit(solution)/shard_map/sre,ef->srf/dot_general | solution.py:282
  96.7 21.1 %collective-permute-done.halo_ref = bf16[2,1024,256]{2,1,0:T(8,128)(2,1)S(1)} collective-permute-done((bf16[2,1024,256]{2,1,0:T(8,128)(2,1)S(1)}, bf16[2,1024,256]{2,1,0:T(8,128)(2,1)S(1)}, u32[]{:S(2)}, u32[]{:S(2)}) %collective-permute-start) | collective-permute-done | bytes 1048608 | tf_op jit(solution)/shard_map/ppermute | solution.py:263
  117.7 33.3 %attend.1 = (bf16[2,2048,128]{2,1,0:T(8,128)(2,1)S(1)}, bf16[2,2,2048,128]{3,2,1,0:T(8,128)(2,1)}) custom-call(bf16[2,2048,384]{2,1,0:T(8,128)(2,1)} %copy-done.5, bf16[2,1024,256]{2,1,0:T(8,128)(2,1)S(1)} %collective-permute-done.halo_ref, bf16[2,3072,64]{2,1,0:T(8,128)(2,1)S(1)} %maximum_maximum_fusion.augk_ref, ...), custom_call_target="tpu_custom_call" | custom-call | tf_op jit(solution)/shard_map/attend/pallas_call | solution.py:107
  151.0 9.5 %copy.73 = bf16[2,2048,128]{2,0,1:T(2,128)(2,1)} copy(bf16[2,2048,128]{2,1,0:T(8,128)(2,1)S(1)} %get-tuple-element.19.out_ref) | data formatting | bytes 2097152 | tf_op jit(solution)/shard_map/attend/pallas_call | solution.py:107
  164.6 15.0 %all-to-all-done = bf16[2,2048,128]{2,0,1:T(2,128)(2,1)S(1)} async-done(((bf16[2,2048,128]{2,0,1:T(2,128)(2,1)}), bf16[2,2048,128]{2,0,1:T(2,128)(2,1)S(1)}, u32[]{:S(2)}, u32[]{:S(2)}) %all-to-all-start) | async-done | bytes 1048608 | tf_op jit(solution)/shard_map/all_to_all | solution.py:324
  185.2 10.5 %fusion.62 = f32[2,256,8,512]{3,1,2,0:T(8,128)} fusion(bf16[8,1024,512,1]{2,1,0,3:T(8,128)(2,1)} %bitcast.195, f32[2,256,1024]{2,1,0:T(8,128)S(1)} %get-tuple-element.114, f32[1024]{0:T(1024)S(1)} %get-tuple-element.101, f32[1024]{0:T(1024)S(1)} %get-tuple-element.99, f32[2,256]{1,0:T(2,128)S(1)} %add_rsqrt_fusion, f32[2,256]{1,0:T(2,128)S(1)} %broadcast_multiply_fusion.4), kind=kOutput, calls=%fused_computation.126 | convolution fusion | flops 4297588736 | bytes 18886656 | tf_op jit(solution)/shard_map/sre,gef->gsrf/dot_general | solution.py:282
  195.7 30.2 %all-gather.15.cloned.1.call-done = bf16[4096,1024]{1,0:T(8,128)(2,1)} async-done(((bf16[512,1024]{1,0:T(8,128)(2,1)}), bf16[4096,1024]{1,0:T(8,128)(2,1)}) %all-gather.15.cloned.1.call-update) | async-done | bytes 8388624 | tf_op jit(solution)/shard_map/all_gather | solution.py:305
  226.0 13.6 %convert_reduce_fusion = (f32[8,512]{1,0:T(8,128)S(1)}, bf16[8,2,256,512]{3,2,0,1:T(8,128)(2,1)S(1)}) fusion(f32[2,256,8,512]{3,1,2,0:T(8,128)} %fusion.62, f32[8,512]{1,0:T(8,128)S(1)} %slice_convert_fusion, bf16[8,512,1024,1]{2,1,0,3:T(8,128)(2,1)} %bitcast.193, bf16[2,256,1024]{2,1,0:T(8,128)(2,1)} %param.16), kind=kOutput, calls=%fused_computation.18 | convolution fusion | flops 4343197696 | bytes 22052864 | tf_op jit(solution)/shard_map/srd,gfd->gsrf/dot_general | solution.py:282
  239.6 5.0 fusion.30
  250.0 10.8 %fusion.11 = bf16[8,1024,512]{1,2,0:T(8,128)(2,1)} fusion(bf16[8,2,256,512]{3,2,0,1:T(8,128)(2,1)} %copy-done.23, f32[2,256,1024]{2,1,0:T(8,128)} %copy-done.6, f32[1024]{0:T(1024)S(1)} %get-tuple-element.101, f32[1024]{0:T(1024)S(1)} %get-tuple-element.99, f32[2,256]{1,0:T(2,128)S(1)} %add_rsqrt_fusion, f32[2,256]{1,0:T(2,128)S(1)} %broadcast_multiply_fusion.4), kind=kOutput, calls=%fused_computation.21 | convolution fusion | flops 4301783040 | bytes 14692352 | tf_op jit(solution)/shard_map/sre,gsrf->gef/dot_general | solution.py:282
  261.1 13.4 %bitcast_convert_fusion = bf16[8,512,1024]{2,1,0:T(8,128)(2,1)} fusion(bf16[2,256,1024]{2,1,0:T(8,128)(2,1)} %param.16, f32[2,256,8,512]{3,1,2,0:T(8,128)} %fusion.62, f32[8,512]{1,0:T(8,128)S(1)} %slice_convert_fusion), kind=kOutput, calls=%fused_computation | convolution fusion | flops 4320133120 | bytes 17842176 | tf_op jit(solution)/shard_map/gsrf,srd->gfd/dot_general | solution.py:282
  282.1 20.3 %all_to_all.36 = bf16[2,256,1024]{1,0,2:T(2,128)(2,1)} all-to-all(bf16[2,256,1024]{1,0,2:T(2,128)(2,1)} %copy.76), channel_id=1, replica_groups=mesh['seq'=4,'fsdp'=8] {'fsdp'}, dimensions={2} | all-to-all | bytes 2097152 | tf_op jit(solution)/shard_map/all_to_all | solution.py:348
  306.1 41.1 %attend_back.1 = (bf16[2,2048,128]{2,1,0:T(8,128)(2,1)}, f32[2,2048,256]{2,1,0:T(8,128)}, bf16[2,1024,256]{2,1,0:T(8,128)(2,1)}) custom-call(bf16[2,2048,384]{2,1,0:T(8,128)(2,1)} %copy-done.5, bf16[2,1024,256]{2,1,0:T(8,128)(2,1)} %copy-done.2, bf16[2,3072,64]{2,1,0:T(8,128)(2,1)} %copy-done, bf16[2,2,2048,128]{3,2,1,0:T(8,128)(2,1)} %get-tuple-element.20.q2_ref, ...), custom_call_target="tpu_custom_call" | custom-call | tf_op jit(solution)/shard_map/attend_back/pallas_call | solution.py:191
  348.7 24.4 %collective-permute-done.1 = bf16[2,1024,256]{2,1,0:T(8,128)(2,1)S(1)} collective-permute-done((bf16[2,1024,256]{2,1,0:T(8,128)(2,1)}, bf16[2,1024,256]{2,1,0:T(8,128)(2,1)S(1)}, u32[]{:S(2)}, u32[]{:S(2)}) %collective-permute-start.1) | collective-permute-done | bytes 1048608 | tf_op jit(solution)/shard_map/ppermute | solution.py:263
  377.1 7.1 %convolution_convert_fusion = bf16[2,2048,1024]{2,1,0:T(8,128)(2,1)} fusion(bf16[2,2048,128]{2,1,0:T(8,128)(2,1)S(1)} %copy-done.14, bf16[2,2048,256]{2,1,0:T(8,128)(2,1)S(1)} %add_convert_fusion.1, bf16[1024,128]{1,0:T(8,128)(2,1)S(1)} %copy.71, bf16[1024,256]{1,0:T(8,128)(2,1)S(1)} %copy-done.17), kind=kOutput, calls=%fused_computation.22 | convolution fusion | flops 3233284096 | bytes 12320768 | tf_op jit(solution)/shard_map/srf,ef->sre/dot_general | solution.py:282
  385.4 13.8 %fusion.32 = bf16[2,256,1024]{2,1,0:T(8,128)(2,1)} fusion(f32[2,256,1024]{2,1,0:T(8,128)} %copy-done.6, bf16[8,512,1024,1]{2,1,0,3:T(8,128)(2,1)} %bitcast.194, f32[1024]{0:T(1024)S(1)} %get-tuple-element.100, f32[2,256,8,512]{3,1,2,0:T(8,128)} %fusion.62, f32[8,512]{1,0:T(8,128)S(1)} %slice_convert_fusion), kind=kOutput, calls=%fused_computation.59 | convolution fusion | flops 4317511680 | bytes 19943424 | tf_op jit(solution)/shard_map/gsrf,gfd->srd/dot_general | solution.py:282
  399.8 7.9 %bitcast_convert_fusion.3 = bf16[1024,384]{1,0:T(8,128)(2,1)} fusion(bf16[2,2048,1024]{2,1,0:T(8,128)(2,1)} %all-gather.9.cloned.1.call-done, bf16[2,2048,128]{2,1,0:T(8,128)(2,1)S(1)} %copy-done.15, bf16[2,2048,256]{2,1,0:T(8,128)(2,1)S(1)} %copy-done.8), kind=kOutput, calls=%fused_computation.72 | convolution fusion | flops 3227910144 | bytes 12320768 | tf_op jit(solution)/shard_map/sre,srf->ef/dot_general | solution.py:282
  407.8 35.6 %reduce-scatter.11.cloned.1.call-done = bf16[1,512,1024]{2,1,0:T(8,128)(2,1)} async-done(((bf16[8,512,1024]{2,1,0:T(8,128)(2,1)}), bf16[1,512,1024]{2,1,0:T(8,128)(2,1)}) %reduce-scatter.11.cloned.1.call-update) | async-done | bytes 1048592 | tf_op jit(solution)/shard_map/reduce_scatter | solution.py:352
  443.6 74.9 %reduce-scatter.5.cloned.1.call-done = bf16[2,256,1024]{2,1,0:T(8,128)(2,1)} async-done(((bf16[2,2048,1024]{2,1,0:T(8,128)(2,1)}), bf16[2,256,1024]{2,1,0:T(8,128)(2,1)}) %reduce-scatter.5.cloned.1.call-update) | async-done | bytes 1048592 | tf_op jit(solution)/shard_map/reduce_scatter | solution.py:363
  521.0 24.7 %all-reduce.3 = f32[8,1280]{1,0:T(8,128)S(1)} all-reduce(f32[8,1280]{1,0:T(8,128)S(1)} %constant_dynamic-update-slice_fusion), channel_id=6, replica_groups=mesh['seq'=4,'fsdp'=8] {'fsdp'}, use_global_device_ids=true, to_apply=%region_16.0.clone | all-reduce | flops 10240 | bytes 81920
  546.3 14.1 %all-reduce.4 = (f32[1280]{0:T(1024)S(1)}, f32[2,128]{1,0:T(2,128)}) all-reduce(f32[1280]{0:T(1024)S(1)} %dynamic-slice_reduce_fusion, f32[2,128]{1,0:T(2,128)S(1)} %pad_maximum_fusion.5), channel_id=1, replica_groups=mesh['seq'=4,'fsdp'=8] {'seq'}, use_global_device_ids=true, to_apply=%region_17.18 | all-reduce | flops 1536 | bytes 12288 | tf_op jit(solution)/shard_map/psum | solution.py:380
  564.5 80.1 %all-reduce.8.cloned.1.call-done = (bf16[1024,384]{1,0:T(8,128)(2,1)}, bf16[1024,512]{0,1:T(8,128)(2,1)}, bf16[128,1024]{1,0:T(8,128)(2,1)}, bf16[512,1024]{1,0:T(8,128)(2,1)}) async-done(((bf16[1024,384]{1,0:T(8,128)(2,1)}, bf16[1024,512]{0,1:T(8,128)(2,1)}, bf16[128,1024]{1,0:T(8,128)(2,1)}, bf16[512,1024]{1,0:T(8,128)(2,1)}), (bf16[1024,384]{1,0:T(8,128)(2,1)}, bf16[1024,512]{0,1:T(8,128)(2,1)}, ...) | async-done | bytes 3145744 | tf_op jit(solution)/shard_map/psum | solution.py:368
  (157 shorter events, 74.4 us)
Async XLA Ops:
  7.2 19.7 %copy-start.3 = (bf16[2,256,1024]{2,1,0:T(8,128)(2,1)S(1)}, bf16[2,256,1024]{2,1,0:T(8,128)(2,1)}, u32[]{:S(2)}) copy-start(bf16[2,256,1024]{2,1,0:T(8,128)(2,1)} %param.15) | copy-start | bytes 3145732
  7.2 76.0 %all-gather.9.cloned.1.call-start = ((), (), s32[]{:S(2)}) async-start(), calls=%async_computation.6 | async-start | bytes 9437184 | tf_op jit(solution)/shard_map/all_gather | solution.py:314
  28.3 153.2 %all-gather.11.cloned.1.call-start = ((), (), s32[]{:S(2)}) async-start(), calls=%async_computation.7 | async-start | bytes 2359296 | tf_op jit(solution)/shard_map/all_gather | solution.py:303
  29.1 156.1 %all-gather.13.cloned.1.call-start = ((), (), s32[]{:S(2)}) async-start(), calls=%async_computation.12 | async-start | bytes 9437184 | tf_op jit(solution)/shard_map/all_gather | solution.py:304
  29.8 196.1 %all-gather.15.cloned.1.call-start = ((), (), s32[]{:S(2)}) async-start(), calls=%async_computation.13 | async-start | bytes 9437184 | tf_op jit(solution)/shard_map/all_gather | solution.py:305
  91.2 4.4 copy-start.5
  91.2 4.0 copy-start.9
  91.3 26.5 %collective-permute-start = (bf16[2,1024,256]{2,1,0:T(8,128)(2,1)S(1)}, bf16[2,1024,256]{2,1,0:T(8,128)(2,1)S(1)}, u32[]{:S(2)}, u32[]{:S(2)}) collective-permute-start(bf16[2,1024,256]{2,1,0:T(8,128)(2,1)S(1)} %slice.123), channel_id=1, source_target_pairs={{0,8},{8,16},{16,24},{1,9},{9,17},{17,25},{2,10},{10,18},{18,26},{... | collective-permute-start | bytes 3145736 | tf_op jit(solution)/shard_map/ppermute | solution.py:263
  96.6 54.4 %copy-start = (bf16[2,3072,64]{2,1,0:T(8,128)(2,1)}, bf16[2,3072,64]{2,1,0:T(8,128)(2,1)S(1)}, u32[]{:S(2)}) copy-start(bf16[2,3072,64]{2,1,0:T(8,128)(2,1)S(1)} %maximum_maximum_fusion.augk_ref) | copy-start | bytes 2359300
  117.7 33.3 %copy-start.2 = (bf16[2,1024,256]{2,1,0:T(8,128)(2,1)}, bf16[2,1024,256]{2,1,0:T(8,128)(2,1)S(1)}, u32[]{:S(2)}) copy-start(bf16[2,1024,256]{2,1,0:T(8,128)(2,1)S(1)} %collective-permute-done.halo_ref) | copy-start | bytes 3145732
  151.0 9.5 %copy-start.1 = (bf16[2,2048,128]{2,1,0:T(8,128)(2,1)}, bf16[2,2048,128]{2,1,0:T(8,128)(2,1)S(1)}, u32[]{:S(2)}) copy-start(bf16[2,2048,128]{2,1,0:T(8,128)(2,1)S(1)} %get-tuple-element.19.out_ref) | copy-start | bytes 3145732
  160.5 19.1 %all-to-all-start = ((bf16[2,2048,128]{2,0,1:T(2,128)(2,1)}), bf16[2,2048,128]{2,0,1:T(2,128)(2,1)S(1)}, u32[]{:S(2)}, u32[]{:S(2)}) async-start(bf16[2,2048,128]{2,0,1:T(2,128)(2,1)} %copy.73), calls=%async_computation | async-start | bytes 2097152 | tf_op jit(solution)/shard_map/all_to_all | solution.py:324
  164.1 243.7 %reduce-scatter.7.cloned.1.call-start = ((), (), s32[]{:S(2)}) async-start(), calls=%async_computation.9 | async-start | bytes 2359296 | tf_op jit(solution)/shard_map/reduce_scatter | solution.py:353
  184.8 54.8 %copy-start.6 = (f32[2,256,1024]{2,1,0:T(8,128)}, f32[2,256,1024]{2,1,0:T(8,128)S(1)}, u32[]{:S(2)}) copy-start(f32[2,256,1024]{2,1,0:T(8,128)S(1)} %get-tuple-element.114) | copy-start | bytes 6291460
  226.0 13.6 %copy-start.21 = (bf16[8192,512]{1,0:T(8,128)(2,1)S(1)}, bf16[8192,512]{1,0:T(8,128)(2,1)}, u32[]{:S(2)}) copy-start(bf16[8192,512]{1,0:T(8,128)(2,1)} %all-gather.13.cloned.1.call-done) | copy-start | bytes 25165828
  239.6 5.0 copy-start.23
  239.6 5.0 copy-start.11
  249.9 157.8 %reduce-scatter.9.cloned.1.call-start = ((), (), s32[]{:S(2)}) async-start(), calls=%async_computation.10 | async-start | bytes 9437184 | tf_op jit(solution)/shard_map/reduce_scatter | solution.py:351
  260.8 182.5 %reduce-scatter.11.cloned.1.call-start = ((), (), s32[]{:S(2)}) async-start(), calls=%async_computation.11 | async-start | bytes 9437184 | tf_op jit(solution)/shard_map/reduce_scatter | solution.py:352
  274.5 244.0 %reduce-scatter.5.cloned.1.call-start = ((), (), s32[]{:S(2)}) async-start(), calls=%async_computation.8 | async-start | bytes 9437184 | tf_op jit(solution)/shard_map/reduce_scatter | solution.py:363
  347.2 25.9 %collective-permute-start.1 = (bf16[2,1024,256]{2,1,0:T(8,128)(2,1)}, bf16[2,1024,256]{2,1,0:T(8,128)(2,1)S(1)}, u32[]{:S(2)}, u32[]{:S(2)}) collective-permute-start(bf16[2,1024,256]{2,1,0:T(8,128)(2,1)} %get-tuple-element.22), channel_id=1, source_target_pairs={{8,0},{16,8},{24,16},{9,1},{17,9},{25,17},{10,2},{18,10},{26,18},{... | collective-permute-start | bytes 3145736 | tf_op jit(solution)/shard_map/ppermute | solution.py:263
  384.2 260.5 %all-reduce.8.cloned.1.call-start = ((), (), s32[]{:S(2)}) async-start(), calls=%async_computation.14 | async-start | bytes 6291456 | tf_op jit(solution)/shard_map/psum | solution.py:368
  385.4 13.8 %copy-start.8 = (bf16[2,2048,256]{2,1,0:T(8,128)(2,1)S(1)}, bf16[2,2048,256]{2,1,0:T(8,128)(2,1)}, u32[]{:S(2)}) copy-start(bf16[2,2048,256]{2,1,0:T(8,128)(2,1)} %copy-done.7) | copy-start | bytes 6291460
  385.4 13.8 %copy-start.15 = (bf16[2,2048,128]{2,1,0:T(8,128)(2,1)S(1)}, bf16[2,2048,128]{2,1,0:T(8,128)(2,1)}, u32[]{:S(2)}) copy-start(bf16[2,2048,128]{2,1,0:T(8,128)(2,1)} %get-tuple-element.23) | copy-start | bytes 3145732
  (12 other events, 25.8 us)
Sparse Core Ops, SparseCore 0:
  28.5 54.6 all-gather.8
  85.1 27.8 all-gather.10
  114.9 54.5 all-gather.12
  171.2 54.6 all-gather.14
  250.0 42.0 reduce-scatter.6
  295.8 72.7 reduce-scatter.8
  372.1 71.2 reduce-scatter.10
  447.2 71.2 reduce-scatter.4
  521.7 122.8 all-reduce.7

commit v2 on v1

--- a/solution.py
+++ b/solution.py
@@ -61,9 +61,33 @@
             )
 
 
-def attend_kernel(heads, qkv_ref, halo_ref, augk_ref, augq_ref, out_ref, q2_ref, keys, values, values_t):
-    step = pl.program_id(1)
+def xor(a, b, size):
+    total, bit = 0, 1
+    while bit < size:
+        total = total + bit * lax.rem(lax.div(a, bit) + lax.div(b, bit), 2)
+        bit *= 2
+    return total
+
+
+def enter(peers):
+    barrier = pltpu.get_barrier_semaphore()
+    for peer in peers:
+        pl.semaphore_signal(barrier, inc=1, device_id={"fsdp": peer}, device_id_type=pl.DeviceIdType.MESH)
+    pl.semaphore_wait(barrier, len(peers))
+
+
+def attend_kernel(
+    heads, group, qkv_ref, halo_ref, augk_ref, augq_ref, out_ref, q2_ref, merged_ref,
+    keys, values, values_t, sent, local_sems, send_sems, recv_sems,
+):
+    seq, step = pl.program_id(0), pl.program_id(1)
+    me = lax.axis_index("fsdp")
     nkeys = keys.shape[1]
+    place = xor(me, step, group)
+
+    @pl.when((seq == 0) & (step == 0))
+    def _():
+        enter([xor(me, k, group) for k in range(1, group)])
 
     @pl.when(step == 0)
     def _():
@@ -74,13 +98,13 @@
 
     mask = edge_mask()
     tiles = WINDOW // BLK + 1
-    start = pl.multiple_of(step * BLK, BLK)
+    start = pl.multiple_of(place * BLK, BLK)
     lane = lax.broadcasted_iota(jnp.int32, (BLK, 2 * HD), 1)
     lse_lane = augq_ref.shape[2] + HD - 3
     for h in range(heads):
         qc = heads * 2 * HD + h * HD
-        q = jnp.concatenate([qkv_ref[0, pl.ds(start, BLK), qc : qc + HD] * 0.125, augq_ref[0]], axis=1)
-        scores = [nt(keys[h, pl.ds(start + b * BLK, BLK), :], q) for b in range(tiles)]
+        q = jnp.concatenate([qkv_ref[0, pl.ds(start, BLK), qc : qc + HD] * 0.125, augq_ref[0, pl.ds(start, BLK), :]], axis=1)
+        scores = [nt(keys[h, pl.ds(pl.multiple_of(start + b * BLK, BLK), BLK), :], q) for b in range(tiles)]
         scores = merge_edges(mask, scores)
         peak = functools.reduce(jnp.maximum, scores)
         peak = jnp.max(peak, axis=0, keepdims=True)
@@ -91,42 +115,79 @@
         sub = lax.broadcasted_iota(jnp.int32, total.shape, 0)
         total = jnp.where(sub == HD + 1, peak, total).T
         norm = total[:, HD : HD + 1]
-        out_ref[0, :, h * HD : (h + 1) * HD] = (total[:, :HD] / norm).astype(out_ref.dtype)
+        part = (total[:, :HD] / norm).astype(out_ref.dtype)
+        out_ref[0, pl.ds(start, BLK), h * HD : (h + 1) * HD] = part
+        sent[seq, step, :, h * HD : (h + 1) * HD] = part
         lse = total[:, HD + 1 : HD + 2] + jnp.log(norm)
         hi, mid, low = split3(-lse)
         q2 = q.astype(jnp.float32)
         q2 = jnp.where(lane == lse_lane, hi, q2)
         q2 = jnp.where(lane == lse_lane + 1, mid, q2)
         q2 = jnp.where(lane == lse_lane + 2, low, q2)
-        q2_ref[0, h] = q2.astype(jnp.bfloat16)
-
-
-def attend(qkv, halo, augk, augq, heads):
+        q2_ref[0, h, pl.ds(start, BLK), :] = q2.astype(jnp.bfloat16)
+
+    def own(s):
+        return pltpu.make_async_copy(sent.at[s, 0], merged_ref.at[0, s], local_sems.at[s])
+
+    def away(s, k):
+        return pltpu.make_async_remote_copy(
+            src_ref=sent.at[s, k],
+            dst_ref=merged_ref.at[k, s],
+            send_sem=send_sems.at[s, k],
+            recv_sem=recv_sems.at[s, k],
+            device_id={"fsdp": xor(me, k, group)},
+            device_id_type=pl.DeviceIdType.MESH,
+        )
+
+    @pl.when(step == 0)
+    def _():
+        own(seq).start()
+
+    @pl.when(step > 0)
+    def _():
+        away(seq, step).start()
+
+    @pl.when((seq == pl.num_programs(0) - 1) & (step == pl.num_programs(1) - 1))
+    def _():
+        for s in range(merged_ref.shape[1]):
+            own(s).wait()
+            for k in range(1, group):
+                away(s, k).wait()
+
+
+def attend(qkv, halo, augk, augq, heads, group):
     seqs, rows, cols = qkv.shape
     ext = augk.shape[1]
+    assert rows // BLK == group
     return pl.pallas_call(
-        functools.partial(attend_kernel, heads),
+        functools.partial(attend_kernel, heads, group),
         grid=(seqs, rows // BLK),
         in_specs=[
             pl.BlockSpec((1, rows, cols), lambda s, i: (s, 0, 0)),
             pl.BlockSpec((1, WINDOW, heads * 2 * HD), lambda s, i: (s, 0, 0)),
             pl.BlockSpec((1, ext, HD), lambda s, i: (s, 0, 0)),
-            pl.BlockSpec((1, BLK, HD), lambda s, i: (s, i, 0)),
+            pl.BlockSpec((1, rows, HD), lambda s, i: (s, 0, 0)),
         ],
         out_specs=[
-            pl.BlockSpec((1, BLK, heads * HD), lambda s, i: (s, i, 0)),
-            pl.BlockSpec((1, heads, BLK, 2 * HD), lambda s, i: (s, 0, i, 0)),
+            pl.BlockSpec((1, rows, heads * HD), lambda s, i: (s, 0, 0)),
+            pl.BlockSpec((1, heads, rows, 2 * HD), lambda s, i: (s, 0, 0, 0)),
+            pl.BlockSpec(memory_space=pl.ANY),
         ],
         out_shape=[
             jax.ShapeDtypeStruct((seqs, rows, heads * HD), jnp.bfloat16),
             jax.ShapeDtypeStruct((seqs, heads, rows, 2 * HD), jnp.bfloat16),
+            jax.ShapeDtypeStruct((group, seqs, BLK, heads * HD), jnp.bfloat16),
         ],
         scratch_shapes=[
             pltpu.VMEM((heads, ext, 2 * HD), jnp.bfloat16),
             pltpu.VMEM((heads, ext, 2 * HD), jnp.bfloat16),
             pltpu.VMEM((heads, 2 * HD, ext), jnp.bfloat16),
-        ],
-        compiler_params=pltpu.CompilerParams(vmem_limit_bytes=48 * 2**20),
+            pltpu.VMEM((seqs, group, BLK, heads * HD), jnp.bfloat16),
+            pltpu.SemaphoreType.DMA((seqs,)),
+            pltpu.SemaphoreType.DMA((seqs, group)),
+            pltpu.SemaphoreType.DMA((seqs, group)),
+        ],
+        compiler_params=pltpu.CompilerParams(vmem_limit_bytes=48 * 2**20, collective_id=1, has_side_effects=True),
         name="attend",
     )(qkv, halo, augk, augq)
 
@@ -320,8 +381,9 @@
     packed_bias = pack_columns(head_bias, heads)
     qkv = (dot("sre,ef->srf", normed1, packed_weight) + packed_bias).astype(jnp.bfloat16)
     halo = from_behind(qkv[:, part_rows - WINDOW :, : heads * 2 * HD], "seq", 1)
-    head_out, q2 = attend(qkv, halo, augk, augq, heads)
-    merged = lax.all_to_all(head_out, "fsdp", split_axis=1, concat_axis=2, tiled=True)
+    head_out, q2, merged = attend(qkv, halo, augk, augq, heads, group)
+    me = lax.axis_index("fsdp")
+    merged = jnp.stack([lax.dynamic_index_in_dim(merged, xor(me, k, group), 0, False) for k in range(group)], axis=2).reshape(seqs, local_rows, width)
     resid = x + dot("sre,ef->srf", merged, out_all) + out_off
     z2, rate2 = standardize(resid)
     normed2 = (z2 * gain2 + offset2).astype(jnp.bfloat16)

time: 668 us -> 674 us (level)
  Pallas kernels: 74.3 us -> 83.7 us
    all_gather x1, waiting for transfers between devices: 30.2 us -> 46 us  [body(): proj_all = lax.all_gather(proj_weight, 'fsdp')]
    all_to_all x1 -> x0, waiting for transfers between devices: 15 us -> none  [body(): lax.all_to_all(head_out, 'fsdp', split_axis=1, concat_axis=2, tiled=True)]
    pallas_call x1 -> x0, local copies, waits for them, and re-layouts: 9.46 us -> none  [attend(): pl.pallas_call(functools.partial(attend_kernel, heads), grid=(seqs, rows...]
    pallas_call x1, Pallas kernels: 33.3 us -> 42.7 us  [attend(): pl.pallas_call(functools.partial(attend_kernel, heads, group), grid=(seqs...]
    all_gather x1, waiting for transfers between devices: 0.02 us -> 7.93 us  [body(): fc_all = lax.all_gather(fc_weight, 'fsdp')]
    unnamed x66 -> x79, local copies, waits for them, and re-layouts: 12.3 us -> 16.1 us
  transfers between devices with their start and end apart: 12 -> 11, of which waited for: 8 -> 8; matrix products, arithmetic and copies ran while one was open for 18% -> 16% of each run, Pallas kernels for 11% -> 13%
where the time goes in v2:
time: 674 us; the launch traced here: 668 us
  waiting for transfers between devices  336 us (50%)
  matrix products  99.7 us (15%)
  Pallas kernels  83.7 us (12%)
  blocking collectives  69.8 us (10%)
  local copies, waits for them, and re-layouts  32.1 us (5%)
  other arithmetic  26.1 us (4%)
  between operations  14.9 us (2%)
    dot_general x12, matrix products, dot(): return jnp.einsum(subscripts, a, b, preferred_element_type=jnp.float32)  99.7 us
    psum x1, waiting for transfers between devices, body(): qkv_grad = lax.psum(qkv_grad.astype(low), 'seq').astype(jnp.float32)  80.1 us
    reduce_scatter x1, waiting for transfers between devices, body(): lax.psum_scatter(g_norm1, 'fsdp', scatter_dimension=1, tiled=True)  74.9 us
    all_gather x1, waiting for transfers between devices, body(): normed1 = lax.all_gather(normed1, 'fsdp', axis=1, tiled=True)  48.1 us
    all_gather x1, waiting for transfers between devices, body(): proj_all = lax.all_gather(proj_weight, 'fsdp')  46 us
    pallas_call x1, Pallas kernels, attend(): pl.pallas_call(functools.partial(attend_kernel, heads, group), grid=(seqs...  42.7 us
    ppermute x2, waiting for transfers between devices, from_behind(): return lax.ppermute(block, axis, route)  41.3 us
    pallas_call x1, Pallas kernels, attend_back(): pl.pallas_call(functools.partial(attend_back_kernel, heads), grid=(seqs,...  41 us
  transfers between devices with their start and end apart: 11, of which 8 were waited for; matrix products, arithmetic and copies ran while one was open for 16% of the time, Pallas kernels for 13%

profile of v2, /device:TPU:0, one launch (start us, length us, event | category | flops | bytes accessed | tf_op | source)
XLA Modules:
  0.0 667.9 jit_solution(4372645644816098674)
XLA Ops:
  13.2 10.6 %all-gather.3 = bf16[8,1,1280]{2,1,0:T(2,128)(2,1)S(1)} all-gather(bf16[1,1,1280]{2,1,0:T(2,128)(2,1)S(1)} %reshape.221), channel_id=2, replica_groups=mesh['seq'=4,'fsdp'=8] {'fsdp'}, dimensions={0}, use_global_device_ids=true | all-gather | bytes 23040 | tf_op jit(solution)/shard_map/all_gather | solution.py:359
  35.1 48.1 %all-gather.9.cloned.1.call-done = bf16[2,2048,1024]{2,1,0:T(8,128)(2,1)} async-done(((bf16[2,256,1024]{2,1,0:T(8,128)(2,1)}), bf16[2,2048,1024]{2,1,0:T(8,128)(2,1)}) %all-gather.9.cloned.1.call-update) | async-done | bytes 8388624 | tf_op jit(solution)/shard_map/all_gather | solution.py:375
  83.2 8.2 %add_convert_fusion.qkv_ref = bf16[2,2048,384]{2,1,0:T(8,128)(2,1)S(1)} fusion(bf16[2,2048,1024]{2,1,0:T(8,128)(2,1)} %all-gather.9.cloned.1.call-done, f32[384]{0:T(512)S(1)} %pad_maximum_fusion.4, bf16[1024,128]{1,0:T(8,128)(2,1)S(1)} %copy.69, bf16[1024,256]{1,0:T(8,128)(2,1)S(1)} %copy.92), kind=kOutput, calls=%fused_computation.20 | convolution fusion | flops 3225944064 | bytes 12322304 | tf_op jit(solution)/shard_map/sre,ef->srf/dot_general | solution.py:343
  103.7 16.9 %collective-permute-done.halo_ref = bf16[2,1024,256]{2,1,0:T(8,128)(2,1)S(1)} collective-permute-done((bf16[2,1024,256]{2,1,0:T(8,128)(2,1)}, bf16[2,1024,256]{2,1,0:T(8,128)(2,1)S(1)}, u32[]{:S(2)}, u32[]{:S(2)}) %collective-permute-start) | collective-permute-done | bytes 1048608 | tf_op jit(solution)/shard_map/ppermute | solution.py:324
  120.6 42.7 %attend.1 = (bf16[2,2048,128]{2,1,0:T(8,128)(2,1)S(1)}, bf16[2,2,2048,128]{3,2,1,0:T(8,128)(2,1)}, bf16[8,2,256,128]{3,2,1,0:T(8,128)(2,1)S(1)}) custom-call(bf16[2,2048,384]{2,1,0:T(8,128)(2,1)} %copy-done.6, bf16[2,1024,256]{2,1,0:T(8,128)(2,1)S(1)} %collective-permute-done.halo_ref, bf16[2,3072,64]{2,1,0:T(8,128)(2,1)S(1)} %maximum_maximum_fusion.augk_ref, ...), custom_call_target="tpu_custom_call" | custom-call | tf_op jit(solution)/shard_map/attend/pallas_call | solution.py:162
  169.3 7.9 %all-gather.13.cloned.1.call-done = bf16[8192,512]{1,0:T(8,128)(2,1)} async-done(((bf16[1024,512]{1,0:T(8,128)(2,1)}), bf16[8192,512]{1,0:T(8,128)(2,1)}) %all-gather.13.cloned.1.call-update) | async-done | bytes 8388624 | tf_op jit(solution)/shard_map/all_gather | solution.py:365
  177.2 10.2 %fusion.66 = f32[2,256,8,512]{3,1,2,0:T(8,128)} fusion(bf16[8,1024,512,1]{2,1,0,3:T(8,128)(2,1)} %bitcast.215, f32[2,256,1024]{2,1,0:T(8,128)S(1)} %get-tuple-element.116, f32[1024]{0:T(1024)S(1)} %get-tuple-element.103, f32[1024]{0:T(1024)S(1)} %get-tuple-element.101, f32[2,256]{1,0:T(2,128)S(1)} %add_rsqrt_fusion, f32[2,256]{1,0:T(2,128)S(1)} %broadcast_multiply_fusion.4), kind=kOutput, calls=%fused_computation.137 | convolution fusion | flops 4297588736 | bytes 18886656 | tf_op jit(solution)/shard_map/sre,gef->gsrf/dot_general | solution.py:343
  187.4 46.0 %all-gather.15.cloned.1.call-done = bf16[4096,1024]{1,0:T(8,128)(2,1)} async-done(((bf16[512,1024]{1,0:T(8,128)(2,1)}), bf16[4096,1024]{1,0:T(8,128)(2,1)}) %all-gather.15.cloned.1.call-update) | async-done | bytes 8388624 | tf_op jit(solution)/shard_map/all_gather | solution.py:366
  233.5 13.6 %convert_reduce_fusion = (f32[8,512]{1,0:T(8,128)S(1)}, bf16[8,2,256,512]{3,2,0,1:T(8,128)(2,1)S(1)}) fusion(f32[2,256,8,512]{3,1,2,0:T(8,128)} %fusion.66, f32[8,512]{1,0:T(8,128)S(1)} %slice_convert_fusion, bf16[8,512,1024,1]{2,1,0,3:T(8,128)(2,1)} %bitcast.213, bf16[2,256,1024]{2,1,0:T(8,128)(2,1)} %param.16), kind=kOutput, calls=%fused_computation.18 | convolution fusion | flops 4343197696 | bytes 22052864 | tf_op jit(solution)/shard_map/srd,gfd->gsrf/dot_general | solution.py:343
  247.1 4.9 fusion.30
  257.4 10.8 %fusion.11 = bf16[8,1024,512]{1,2,0:T(8,128)(2,1)} fusion(bf16[8,2,256,512]{3,2,0,1:T(8,128)(2,1)} %copy-done.26, f32[2,256,1024]{2,1,0:T(8,128)} %copy-done.7, f32[1024]{0:T(1024)S(1)} %get-tuple-element.103, f32[1024]{0:T(1024)S(1)} %get-tuple-element.101, f32[2,256]{1,0:T(2,128)S(1)} %add_rsqrt_fusion, f32[2,256]{1,0:T(2,128)S(1)} %broadcast_multiply_fusion.4), kind=kOutput, calls=%fused_computation.21 | convolution fusion | flops 4301783040 | bytes 14692352 | tf_op jit(solution)/shard_map/sre,gsrf->gef/dot_general | solution.py:343
  268.6 13.4 %bitcast_convert_fusion = bf16[8,512,1024]{2,1,0:T(8,128)(2,1)} fusion(bf16[2,256,1024]{2,1,0:T(8,128)(2,1)} %param.16, f32[2,256,8,512]{3,1,2,0:T(8,128)} %fusion.66, f32[8,512]{1,0:T(8,128)S(1)} %slice_convert_fusion), kind=kOutput, calls=%fused_computation | convolution fusion | flops 4320133120 | bytes 17842176 | tf_op jit(solution)/shard_map/gsrf,srd->gfd/dot_general | solution.py:343
  282.1 3.8 fusion.38
  289.6 20.4 %all_to_all.18 = bf16[2,256,1024]{1,0,2:T(2,128)(2,1)} all-to-all(bf16[2,256,1024]{1,0,2:T(2,128)(2,1)} %copy.73), channel_id=1, replica_groups=mesh['seq'=4,'fsdp'=8] {'fsdp'}, dimensions={2} | all-to-all | bytes 2097152 | tf_op jit(solution)/shard_map/all_to_all | solution.py:410
  313.6 41.0 %attend_back.1 = (bf16[2,2048,128]{2,1,0:T(8,128)(2,1)}, f32[2,2048,256]{2,1,0:T(8,128)}, bf16[2,1024,256]{2,1,0:T(8,128)(2,1)}) custom-call(bf16[2,2048,384]{2,1,0:T(8,128)(2,1)} %copy-done.6, bf16[2,1024,256]{2,1,0:T(8,128)(2,1)} %copy-done.1, bf16[2,3072,64]{2,1,0:T(8,128)(2,1)} %copy-done, bf16[2,2,2048,128]{3,2,1,0:T(8,128)(2,1)} %get-tuple-element.21.q2_ref, ...), custom_call_target="tpu_custom_call" | custom-call | tf_op jit(solution)/shard_map/attend_back/pallas_call | solution.py:252
  356.2 24.4 %collective-permute-done.1 = bf16[2,1024,256]{2,1,0:T(8,128)(2,1)S(1)} collective-permute-done((bf16[2,1024,256]{2,1,0:T(8,128)(2,1)}, bf16[2,1024,256]{2,1,0:T(8,128)(2,1)S(1)}, u32[]{:S(2)}, u32[]{:S(2)}) %collective-permute-start.1) | collective-permute-done | bytes 1048608 | tf_op jit(solution)/shard_map/ppermute | solution.py:324
  384.6 7.1 %convolution_convert_fusion = bf16[2,2048,1024]{2,1,0:T(8,128)(2,1)} fusion(bf16[2,2048,128]{2,1,0:T(8,128)(2,1)S(1)} %copy-done.14, bf16[2,2048,256]{2,1,0:T(8,128)(2,1)S(1)} %add_convert_fusion.1, bf16[1024,128]{1,0:T(8,128)(2,1)S(1)} %copy.69, bf16[1024,256]{1,0:T(8,128)(2,1)S(1)} %copy-done.18), kind=kOutput, calls=%fused_computation.22 | convolution fusion | flops 3233284096 | bytes 12320768 | tf_op jit(solution)/shard_map/srf,ef->sre/dot_general | solution.py:343
  392.9 13.8 %fusion.32 = bf16[2,256,1024]{2,1,0:T(8,128)(2,1)} fusion(f32[2,256,1024]{2,1,0:T(8,128)} %copy-done.7, bf16[8,512,1024,1]{2,1,0,3:T(8,128)(2,1)} %bitcast.214, f32[1024]{0:T(1024)S(1)} %get-tuple-element.102, f32[2,256,8,512]{3,1,2,0:T(8,128)} %fusion.66, f32[8,512]{1,0:T(8,128)S(1)} %slice_convert_fusion), kind=kOutput, calls=%fused_computation.59 | convolution fusion | flops 4317511680 | bytes 19943424 | tf_op jit(solution)/shard_map/gsrf,gfd->srd/dot_general | solution.py:343
  407.4 7.9 %bitcast_convert_fusion.3 = bf16[1024,384]{1,0:T(8,128)(2,1)} fusion(bf16[2,2048,1024]{2,1,0:T(8,128)(2,1)} %all-gather.9.cloned.1.call-done, bf16[2,2048,128]{2,1,0:T(8,128)(2,1)S(1)} %copy-done.15, bf16[2,2048,256]{2,1,0:T(8,128)(2,1)S(1)} %copy-done.9), kind=kOutput, calls=%fused_computation.72 | convolution fusion | flops 3227910144 | bytes 12320768 | tf_op jit(solution)/shard_map/sre,srf->ef/dot_general | solution.py:343
  415.3 35.6 %reduce-scatter.11.cloned.1.call-done = bf16[1,512,1024]{2,1,0:T(8,128)(2,1)} async-done(((bf16[8,512,1024]{2,1,0:T(8,128)(2,1)}), bf16[1,512,1024]{2,1,0:T(8,128)(2,1)}) %reduce-scatter.11.cloned.1.call-update) | async-done | bytes 1048592 | tf_op jit(solution)/shard_map/reduce_scatter | solution.py:414
  451.2 74.9 %reduce-scatter.5.cloned.1.call-done = bf16[2,256,1024]{2,1,0:T(8,128)(2,1)} async-done(((bf16[2,2048,1024]{2,1,0:T(8,128)(2,1)}), bf16[2,256,1024]{2,1,0:T(8,128)(2,1)}) %reduce-scatter.5.cloned.1.call-update) | async-done | bytes 1048592 | tf_op jit(solution)/shard_map/reduce_scatter | solution.py:425
  528.5 24.7 %all-reduce.3 = f32[8,1280]{1,0:T(8,128)S(1)} all-reduce(f32[8,1280]{1,0:T(8,128)S(1)} %constant_dynamic-update-slice_fusion), channel_id=6, replica_groups=mesh['seq'=4,'fsdp'=8] {'fsdp'}, use_global_device_ids=true, to_apply=%region_16.17.clone | all-reduce | flops 10240 | bytes 81920
  553.9 14.1 %all-reduce.4 = (f32[1280]{0:T(1024)S(1)}, f32[2,128]{1,0:T(2,128)}) all-reduce(f32[1280]{0:T(1024)S(1)} %dynamic-slice_reduce_fusion, f32[2,128]{1,0:T(2,128)S(1)} %pad_maximum_fusion.5), channel_id=1, replica_groups=mesh['seq'=4,'fsdp'=8] {'seq'}, use_global_device_ids=true, to_apply=%region_17.18 | all-reduce | flops 1536 | bytes 12288 | tf_op jit(solution)/shard_map/psum | solution.py:442
  572.1 80.1 %all-reduce.8.cloned.1.call-done = (bf16[1024,384]{1,0:T(8,128)(2,1)}, bf16[1024,512]{0,1:T(8,128)(2,1)}, bf16[128,1024]{1,0:T(8,128)(2,1)}, bf16[512,1024]{1,0:T(8,128)(2,1)}) async-done(((bf16[1024,384]{1,0:T(8,128)(2,1)}, bf16[1024,512]{0,1:T(8,128)(2,1)}, bf16[128,1024]{1,0:T(8,128)(2,1)}, bf16[512,1024]{1,0:T(8,128)(2,1)}), (bf16[1024,384]{1,0:T(8,128)(2,1)}, bf16[1024,512]{0,1:T(8,128)(2,1)}, ...) | async-done | bytes 3145744 | tf_op jit(solution)/shard_map/psum | solution.py:430
  (166 shorter events, 71.6 us)
Async XLA Ops:
  7.2 19.7 %copy-start.4 = (bf16[2,256,1024]{2,1,0:T(8,128)(2,1)S(1)}, bf16[2,256,1024]{2,1,0:T(8,128)(2,1)}, u32[]{:S(2)}) copy-start(bf16[2,256,1024]{2,1,0:T(8,128)(2,1)} %param.15) | copy-start | bytes 3145732
  7.2 76.0 %all-gather.9.cloned.1.call-start = ((), (), s32[]{:S(2)}) async-start(), calls=%async_computation.5 | async-start | bytes 9437184 | tf_op jit(solution)/shard_map/all_gather | solution.py:375
  28.3 136.3 %all-gather.11.cloned.1.call-start = ((), (), s32[]{:S(2)}) async-start(), calls=%async_computation.6 | async-start | bytes 2359296 | tf_op jit(solution)/shard_map/all_gather | solution.py:364
  29.1 148.2 %all-gather.13.cloned.1.call-start = ((), (), s32[]{:S(2)}) async-start(), calls=%async_computation.11 | async-start | bytes 9437184 | tf_op jit(solution)/shard_map/all_gather | solution.py:365
  29.8 203.6 %all-gather.15.cloned.1.call-start = ((), (), s32[]{:S(2)}) async-start(), calls=%async_computation.12 | async-start | bytes 9437184 | tf_op jit(solution)/shard_map/all_gather | solution.py:366
  30.4 384.9 %reduce-scatter.7.cloned.1.call-start = ((), (), s32[]{:S(2)}) async-start(), calls=%async_computation.8 | async-start | bytes 2359296 | tf_op jit(solution)/shard_map/reduce_scatter | solution.py:415
  31.4 51.8 %copy-start.17 = (bf16[1024,256]{1,0:T(8,128)(2,1)}, bf16[1024,256]{1,0:T(8,128)(2,1)S(1)}, u32[]{:S(2)}) copy-start(bf16[1024,256]{1,0:T(8,128)(2,1)S(1)} %copy.92) | copy-start | bytes 1572868
  93.1 4.5 copy-start.10
  94.1 26.5 %collective-permute-start = (bf16[2,1024,256]{2,1,0:T(8,128)(2,1)}, bf16[2,1024,256]{2,1,0:T(8,128)(2,1)S(1)}, u32[]{:S(2)}, u32[]{:S(2)}) collective-permute-start(bf16[2,1024,256]{2,1,0:T(8,128)(2,1)} %slice.123), channel_id=1, source_target_pairs={{0,8},{8,16},{16,24},{1,9},{9,17},{17,25},{2,10},{10,18},{18,26},{... | collective-permute-start | bytes 3145736 | tf_op jit(solution)/shard_map/ppermute | solution.py:324
  101.1 19.5 %copy-start.2 = (bf16[2,2048,64]{2,1,0:T(8,128)(2,1)S(1)}, bf16[2,2048,64]{2,1,0:T(8,128)(2,1)}, u32[]{:S(2)}) copy-start(bf16[2,2048,64]{2,1,0:T(8,128)(2,1)} %maximum_maximum_fusion.1.augq_ref) | copy-start | bytes 1572868
  103.7 59.6 %copy-start = (bf16[2,3072,64]{2,1,0:T(8,128)(2,1)}, bf16[2,3072,64]{2,1,0:T(8,128)(2,1)S(1)}, u32[]{:S(2)}) copy-start(bf16[2,3072,64]{2,1,0:T(8,128)(2,1)S(1)} %maximum_maximum_fusion.augk_ref) | copy-start | bytes 2359300
  120.6 42.7 %copy-start.1 = (bf16[2,1024,256]{2,1,0:T(8,128)(2,1)}, bf16[2,1024,256]{2,1,0:T(8,128)(2,1)S(1)}, u32[]{:S(2)}) copy-start(bf16[2,1024,256]{2,1,0:T(8,128)(2,1)S(1)} %collective-permute-done.halo_ref) | copy-start | bytes 3145732
  168.9 78.2 %copy-start.7 = (f32[2,256,1024]{2,1,0:T(8,128)}, f32[2,256,1024]{2,1,0:T(8,128)S(1)}, u32[]{:S(2)}) copy-start(f32[2,256,1024]{2,1,0:T(8,128)S(1)} %get-tuple-element.116) | copy-start | bytes 6291460
  233.5 13.6 %copy-start.24 = (bf16[8192,512]{1,0:T(8,128)(2,1)S(1)}, bf16[8192,512]{1,0:T(8,128)(2,1)}, u32[]{:S(2)}) copy-start(bf16[8192,512]{1,0:T(8,128)(2,1)} %all-gather.13.cloned.1.call-done) | copy-start | bytes 25165828
  247.1 5.0 copy-start.26
  247.1 5.0 copy-start.12
  257.4 157.9 %reduce-scatter.9.cloned.1.call-start = ((), (), s32[]{:S(2)}) async-start(), calls=%async_computation.9 | async-start | bytes 9437184 | tf_op jit(solution)/shard_map/reduce_scatter | solution.py:413
  268.3 182.6 %reduce-scatter.11.cloned.1.call-start = ((), (), s32[]{:S(2)}) async-start(), calls=%async_computation.10 | async-start | bytes 9437184 | tf_op jit(solution)/shard_map/reduce_scatter | solution.py:414
  282.0 244.1 %reduce-scatter.5.cloned.1.call-start = ((), (), s32[]{:S(2)}) async-start(), calls=%async_computation.7 | async-start | bytes 9437184 | tf_op jit(solution)/shard_map/reduce_scatter | solution.py:425
  354.6 26.0 %collective-permute-start.1 = (bf16[2,1024,256]{2,1,0:T(8,128)(2,1)}, bf16[2,1024,256]{2,1,0:T(8,128)(2,1)S(1)}, u32[]{:S(2)}, u32[]{:S(2)}) collective-permute-start(bf16[2,1024,256]{2,1,0:T(8,128)(2,1)} %get-tuple-element.24), channel_id=1, source_target_pairs={{8,0},{16,8},{24,16},{9,1},{17,9},{25,17},{10,2},{18,10},{26,18},{... | collective-permute-start | bytes 3145736 | tf_op jit(solution)/shard_map/ppermute | solution.py:324
  380.6 4.0 copy-start.18
  391.7 260.5 %all-reduce.8.cloned.1.call-start = ((), (), s32[]{:S(2)}) async-start(), calls=%async_computation.13 | async-start | bytes 6291456 | tf_op jit(solution)/shard_map/psum | solution.py:430
  392.9 13.8 %copy-start.9 = (bf16[2,2048,256]{2,1,0:T(8,128)(2,1)S(1)}, bf16[2,2048,256]{2,1,0:T(8,128)(2,1)}, u32[]{:S(2)}) copy-start(bf16[2,2048,256]{2,1,0:T(8,128)(2,1)} %copy-done.8) | copy-start | bytes 6291460
  392.9 13.8 %copy-start.15 = (bf16[2,2048,128]{2,1,0:T(8,128)(2,1)S(1)}, bf16[2,2048,128]{2,1,0:T(8,128)(2,1)}, u32[]{:S(2)}) copy-start(bf16[2,2048,128]{2,1,0:T(8,128)(2,1)} %get-tuple-element.25) | copy-start | bytes 3145732
  (14 other events, 24.3 us)
Sparse Core Ops, SparseCore 0:
  28.5 54.6 all-gather.8
  85.1 27.8 all-gather.10
  114.9 62.2 all-gather.12
  179.0 54.4 all-gather.14
  257.5 42.0 reduce-scatter.6
  303.3 72.7 reduce-scatter.8
  379.6 71.2 reduce-scatter.10
  454.8 71.2 reduce-scatter.4
  529.3 122.8 all-reduce.7

commit v3 on v2

--- a/solution.py
+++ b/solution.py
@@ -1,9 +1,28 @@
 import functools
-import jax, jax.numpy as jnp
+import math
+
+import jax
+import jax.numpy as jnp
 from jax import lax
 from jax.experimental import pallas as pl
 from jax.experimental.pallas import tpu as pltpu
 from jax.sharding import PartitionSpec as P
+
+
+def standardize(values):
+    centre = values - jnp.mean(values, axis=-1, keepdims=True)
+    spread = jnp.mean(centre * centre, axis=-1, keepdims=True)
+    rate = lax.rsqrt(spread + norm_eps)
+    return centre * rate, rate
+
+
+def norm_grad(direction, z, rate):
+    mean_d = jnp.mean(direction, axis=-1, keepdims=True)
+    mean_dz = jnp.mean(direction * z, axis=-1, keepdims=True)
+    return rate * (direction - mean_d - z * mean_dz)
+
+
+norm_eps = 1e-05
 
 HD = 64
 WINDOW = 1024
@@ -43,22 +62,6 @@
     rows = lax.broadcasted_iota(jnp.int32, (BLK, BLK), 0)
     cols = lax.broadcasted_iota(jnp.int32, (BLK, BLK), 1)
     return rows > cols
-
-
-def fill_keys(heads, qkv_ref, halo_ref, augk_ref, keys, values):
-    halo_rows = halo_ref.shape[1]
-    rows = qkv_ref.shape[1]
-    ones = jnp.ones((1, HD), jnp.bfloat16)
-    for h in range(heads):
-        c = h * 2 * HD
-        for source, base, size in ((halo_ref, 0, halo_rows), (qkv_ref, halo_rows, rows)):
-            pair = source[0, :, c : c + 2 * HD]
-            keys[h, base : base + size, :] = jnp.concatenate(
-                [pair[:, :HD], augk_ref[0, base : base + size, :]], axis=1
-            )
-            values[h, base : base + size, :] = jnp.concatenate(
-                [pair[:, HD:], jnp.broadcast_to(ones, (size, HD))], axis=1
-            )
 
 
 def xor(a, b, size):
@@ -69,127 +72,256 @@
     return total
 
 
+MESH = pl.DeviceIdType.MESH
+SLOT_AT = (1, 3, 5, 2, 4, 0, 7, 6)
+STEP_OF = tuple(SLOT_AT.index(r) for r in range(8))
+NEAR = 6
+
+
 def enter(peers):
     barrier = pltpu.get_barrier_semaphore()
     for peer in peers:
-        pl.semaphore_signal(barrier, inc=1, device_id={"fsdp": peer}, device_id_type=pl.DeviceIdType.MESH)
+        pl.semaphore_signal(barrier, inc=1, device_id={"fsdp": peer}, device_id_type=MESH)
     pl.semaphore_wait(barrier, len(peers))
 
 
 def attend_kernel(
-    heads, group, qkv_ref, halo_ref, augk_ref, augq_ref, out_ref, q2_ref, merged_ref,
-    keys, values, values_t, sent, local_sems, send_sems, recv_sems,
+    heads, group, qkv_ref, augk_ref, augq_ref, out_w, fc_w, proj_w,
+    out_ref, q2_ref, halo_ref, merged_ref, out_all, fc_all, proj_all,
+    keys, values, values_t, sent, behind, own_sems, send_sems, recv_sems, halo_sems, w_own, w_send, w_recv,
 ):
-    seq, step = pl.program_id(0), pl.program_id(1)
+    step = pl.program_id(0)
+    last = pl.num_programs(0) - 1
     me = lax.axis_index("fsdp")
-    nkeys = keys.shape[1]
-    place = xor(me, step, group)
-
-    @pl.when((seq == 0) & (step == 0))
-    def _():
-        enter([xor(me, k, group) for k in range(1, group)])
+    line = lax.axis_index("seq")
+    line_end = lax.axis_size("seq") - 1
+    at = [xor(me, k, group) for k in range(group)]
+    seqs, rows = qkv_ref.shape[0], qkv_ref.shape[1]
+    half = group // 2
+    seq = lax.rem(lax.div(step, half), 2)
+    lower = lax.div(step, group)
+    place = (1 - lower) * half + lax.rem(step + me, half)
+    width = heads * 2 * HD
+    low = jnp.bfloat16
+
+    def halo_copy():
+        return pltpu.make_async_remote_copy(
+            src_ref=qkv_ref.at[:, pl.ds(rows - WINDOW, WINDOW), pl.ds(0, width)],
+            dst_ref=behind, send_sem=halo_sems.at[0], recv_sem=halo_sems.at[1],
+            device_id={"seq": lax.rem(line + 1, line_end + 1)}, device_id_type=MESH,
+        )
+
+    weights = ((out_w, out_all, False), (fc_w, fc_all, True), (proj_w, proj_all, True))
+
+    def slot(a, r):
+        return weights[a][1].at[STEP_OF[r] if weights[a][2] else r]
+
+    def w_copy(a, r, second=False):
+        to = at[1] if r % 2 else at[r]
+        src = weights[a][0] if r in (1, 2, 4) else slot(a, r - 1) if r % 2 else None
+        dst, sem = slot(a, r), r
+        if r == 6:
+            size = weights[a][0].shape[0] // 2
+            part = pl.ds(size if second else 0, size)
+            src = slot(a, 4 if second else 2).at[part]
+            to = at[2] if second else at[4]
+            dst, sem = dst.at[part], 0 if second else 6
+        return pltpu.make_async_remote_copy(
+            src_ref=src, dst_ref=dst, send_sem=w_send.at[a, sem], recv_sem=w_recv.at[a, sem],
+            device_id={"fsdp": to}, device_id_type=MESH,
+        )
+
+    def w_keep(a):
+        return pltpu.make_async_copy(weights[a][0], slot(a, 0), w_own.at[a])
+
+    def forward(a):
+        w_copy(a, 2).wait_recv()
+        w_copy(a, 3).start()
+        w_copy(a, 4).wait_recv()
+        w_copy(a, 5).start()
+        if not weights[a][2]:
+            w_copy(a, 6).start()
+            w_copy(a, 6, True).start()
 
     @pl.when(step == 0)
     def _():
-        fill_keys(heads, qkv_ref, halo_ref, augk_ref, keys, values)
-        for h in range(heads):
-            for b in range(nkeys // BLK):
-                values_t[h, :, b * BLK : (b + 1) * BLK] = values[h, b * BLK : (b + 1) * BLK, :].T
+        barrier = pltpu.get_barrier_semaphore()
+        for peer in at[1:]:
+            pl.semaphore_signal(barrier, inc=1, device_id={"fsdp": peer}, device_id_type=MESH)
+
+        pl.semaphore_signal(
+            barrier, inc=1, device_id={"seq": lax.rem(line + line_end, line_end + 1)}, device_id_type=MESH
+        )
+        pl.semaphore_wait(barrier, group)
+
+        @pl.when(line < line_end)
+        def _():
+            halo_copy().start()
+
+        for a in range(3):
+            for r in (2, 4, 1):
+                w_copy(a, r).start()
+            w_keep(a).start()
+        for s in range(seqs):
+            fill_keys(s, heads, qkv_ref, augk_ref, WINDOW, keys, values, values_t, None)
+
+    @pl.when(step == group)
+    def _():
+        @pl.when(line > 0)
+        def _():
+            halo_copy().wait_recv()
+
+        @pl.when(line == 0)
+        def _():
+            behind[...] = jnp.zeros_like(behind)
+
+        halo_ref[...] = behind[...]
+        for s in range(seqs):
+            fill_keys(s, heads, behind, augk_ref, 0, keys, values, values_t, None)
 
     mask = edge_mask()
     tiles = WINDOW // BLK + 1
     start = pl.multiple_of(place * BLK, BLK)
     lane = lax.broadcasted_iota(jnp.int32, (BLK, 2 * HD), 1)
     lse_lane = augq_ref.shape[2] + HD - 3
+    slot_k = xor(me, place, group)
+    spans = [pl.ds(pl.multiple_of(start + b * BLK, BLK), BLK) for b in range(tiles)]
     for h in range(heads):
+        sh = seq * heads + h
         qc = heads * 2 * HD + h * HD
-        q = jnp.concatenate([qkv_ref[0, pl.ds(start, BLK), qc : qc + HD] * 0.125, augq_ref[0, pl.ds(start, BLK), :]], axis=1)
-        scores = [nt(keys[h, pl.ds(pl.multiple_of(start + b * BLK, BLK), BLK), :], q) for b in range(tiles)]
-        scores = merge_edges(mask, scores)
+        q = jnp.concatenate(
+            [qkv_ref[seq, pl.ds(start, BLK), qc : qc + HD] * 0.125, augq_ref[seq, pl.ds(start, BLK), :]], axis=1
+        )
+        scores = merge_edges(mask, [nt(keys[sh, s, :], q) for s in spans])
         peak = functools.reduce(jnp.maximum, scores)
         peak = jnp.max(peak, axis=0, keepdims=True)
-        weights = spread_edges(mask, [jnp.exp(s - peak).astype(jnp.bfloat16) for s in scores])
-        total = sum(
-            nn(values_t[h, :, pl.ds(pl.multiple_of(start + b * BLK, BLK), BLK)], w) for b, w in enumerate(weights)
-        )
+        weights_ = spread_edges(mask, [jnp.exp(s - peak).astype(low) for s in scores])
+        total = sum(nn(values_t[sh, :, s], w) for s, w in zip(spans, weights_))
         sub = lax.broadcasted_iota(jnp.int32, total.shape, 0)
         total = jnp.where(sub == HD + 1, peak, total).T
         norm = total[:, HD : HD + 1]
-        part = (total[:, :HD] / norm).astype(out_ref.dtype)
-        out_ref[0, pl.ds(start, BLK), h * HD : (h + 1) * HD] = part
-        sent[seq, step, :, h * HD : (h + 1) * HD] = part
+        part = (total[:, :HD] / norm).astype(low)
+        out_ref[seq, pl.ds(start, BLK), h * HD : (h + 1) * HD] = part
+        sent[step, :, h * HD : (h + 1) * HD] = part
         lse = total[:, HD + 1 : HD + 2] + jnp.log(norm)
-        hi, mid, low = split3(-lse)
+        hi, mid, lo = split3(-lse)
         q2 = q.astype(jnp.float32)
         q2 = jnp.where(lane == lse_lane, hi, q2)
         q2 = jnp.where(lane == lse_lane + 1, mid, q2)
-        q2 = jnp.where(lane == lse_lane + 2, low, q2)
-        q2_ref[0, h, pl.ds(start, BLK), :] = q2.astype(jnp.bfloat16)
+        q2 = jnp.where(lane == lse_lane + 2, lo, q2)
+        q2_ref[seq, h, pl.ds(start, BLK), :] = q2.astype(low)
+
+    span = sent.shape[2]
+
+    def landing(s, k):
+        return merged_ref.at[s, :, pl.ds(pl.multiple_of(k * span, span), span)]
 
     def own(s):
-        return pltpu.make_async_copy(sent.at[s, 0], merged_ref.at[0, s], local_sems.at[s])
-
-    def away(s, k):
+        return pltpu.make_async_copy(sent.at[step], landing(s, 0), own_sems.at[s])
+
+    def away(s, k, to):
         return pltpu.make_async_remote_copy(
-            src_ref=sent.at[s, k],
-            dst_ref=merged_ref.at[k, s],
-            send_sem=send_sems.at[s, k],
-            recv_sem=recv_sems.at[s, k],
-            device_id={"fsdp": xor(me, k, group)},
-            device_id_type=pl.DeviceIdType.MESH,
+            src_ref=sent.at[step], dst_ref=landing(s, k), send_sem=send_sems.at[s, k], recv_sem=recv_sems.at[s, k],
+            device_id={"fsdp": to}, device_id_type=MESH,
         )
 
-    @pl.when(step == 0)
+    @pl.when(place == me)
     def _():
         own(seq).start()
 
-    @pl.when(step > 0)
+    @pl.when(place != me)
     def _():
-        away(seq, step).start()
-
-    @pl.when((seq == pl.num_programs(0) - 1) & (step == pl.num_programs(1) - 1))
+        away(seq, slot_k, place).start()
+
+    @pl.when(step == last - 3)
     def _():
-        for s in range(merged_ref.shape[1]):
+        forward(0)
+
+    @pl.when(step == last - 1)
+    def _():
+        forward(1)
+
+    @pl.when(step == last)
+    def _():
+        forward(2)
+        w_copy(0, 6).wait_recv()
+        w_copy(0, 6, True).wait_recv()
+        w_copy(0, 7).start()
+        for s in range(seqs):
             own(s).wait()
             for k in range(1, group):
-                away(s, k).wait()
-
-
-def attend(qkv, halo, augk, augq, heads, group):
+                away(s, k, at[k]).wait()
+        for a in range(3):
+            w_keep(a).wait()
+            for r in (1, 2, 3, 4, 5):
+                w_copy(a, r).wait_send()
+            for r in (1, 3, 5):
+                w_copy(a, r).wait_recv()
+        w_copy(0, 6).wait_send()
+        w_copy(0, 6, True).wait_send()
+        w_copy(0, 7).wait()
+
+        @pl.when(line < line_end)
+        def _():
+            halo_copy().wait_send()
+
+
+def fill_keys(s, heads, source, augk_ref, base, keys, values, values_t, keys_t):
+    size = BLK
+    ones = jnp.ones((size, HD), jnp.bfloat16)
+    first = source.shape[1] - WINDOW if base == 0 else 0
+    for h in range(heads):
+        c = h * 2 * HD
+        for i in range(source.shape[1] // size):
+            pair = source[s, i * size : (i + 1) * size, c : c + 2 * HD]
+            span = slice(base + i * size, base + (i + 1) * size)
+            k = jnp.concatenate([pair[:, :HD], augk_ref[s, span, :]], axis=1)
+            v = jnp.concatenate([pair[:, HD:], ones], axis=1)
+            keys[s * heads + h, span, :] = k
+            values[s * heads + h, span, :] = v
+            if values_t is not None:
+                values_t[s * heads + h, :, span] = v.T
+            if keys_t is not None:
+                keys_t[s * heads + h, :, span] = k.T
+
+
+def attend(qkv, augk, augq, out_w, fc_w, proj_w, heads, group):
     seqs, rows, cols = qkv.shape
     ext = augk.shape[1]
     assert rows // BLK == group
+    low = jnp.bfloat16
+    vmem = pl.BlockSpec(memory_space=pltpu.VMEM)
+    hbm = pl.BlockSpec(memory_space=pl.ANY)
+    every = seqs * heads
     return pl.pallas_call(
         functools.partial(attend_kernel, heads, group),
-        grid=(seqs, rows // BLK),
-        in_specs=[
-            pl.BlockSpec((1, rows, cols), lambda s, i: (s, 0, 0)),
-            pl.BlockSpec((1, WINDOW, heads * 2 * HD), lambda s, i: (s, 0, 0)),
-            pl.BlockSpec((1, ext, HD), lambda s, i: (s, 0, 0)),
-            pl.BlockSpec((1, rows, HD), lambda s, i: (s, 0, 0)),
-        ],
-        out_specs=[
-            pl.BlockSpec((1, rows, heads * HD), lambda s, i: (s, 0, 0)),
-            pl.BlockSpec((1, heads, rows, 2 * HD), lambda s, i: (s, 0, 0, 0)),
-            pl.BlockSpec(memory_space=pl.ANY),
-        ],
+        grid=(seqs * rows // BLK,),
+        in_specs=[vmem] * 3 + [hbm] * 3,
+        out_specs=[vmem] * 3 + [hbm] * 4,
         out_shape=[
-            jax.ShapeDtypeStruct((seqs, rows, heads * HD), jnp.bfloat16),
-            jax.ShapeDtypeStruct((seqs, heads, rows, 2 * HD), jnp.bfloat16),
-            jax.ShapeDtypeStruct((group, seqs, BLK, heads * HD), jnp.bfloat16),
-        ],
+            jax.ShapeDtypeStruct((seqs, rows, heads * HD), low),
+            jax.ShapeDtypeStruct((seqs, heads, rows, 2 * HD), low),
+            jax.ShapeDtypeStruct((seqs, WINDOW, heads * 2 * HD), low),
+            jax.ShapeDtypeStruct((seqs, BLK, group * heads * HD), low),
+        ]
+        + [jax.ShapeDtypeStruct((n,) + w.shape, low) for n, w in ((group, out_w), (NEAR, fc_w), (NEAR, proj_w))],
         scratch_shapes=[
-            pltpu.VMEM((heads, ext, 2 * HD), jnp.bfloat16),
-            pltpu.VMEM((heads, ext, 2 * HD), jnp.bfloat16),
-            pltpu.VMEM((heads, 2 * HD, ext), jnp.bfloat16),
-            pltpu.VMEM((seqs, group, BLK, heads * HD), jnp.bfloat16),
+            pltpu.VMEM((every, ext, 2 * HD), low),
+            pltpu.VMEM((every, ext, 2 * HD), low),
+            pltpu.VMEM((every, 2 * HD, ext), low),
+            pltpu.VMEM((seqs * rows // BLK, BLK, heads * HD), low),
+            pltpu.VMEM((seqs, WINDOW, heads * 2 * HD), low),
             pltpu.SemaphoreType.DMA((seqs,)),
             pltpu.SemaphoreType.DMA((seqs, group)),
             pltpu.SemaphoreType.DMA((seqs, group)),
-        ],
-        compiler_params=pltpu.CompilerParams(vmem_limit_bytes=48 * 2**20, collective_id=1, has_side_effects=True),
+            pltpu.SemaphoreType.DMA((2,)),
+            pltpu.SemaphoreType.DMA((3,)),
+            pltpu.SemaphoreType.DMA((3, group)),
+            pltpu.SemaphoreType.DMA((3, group)),
+        ],
+        compiler_params=pltpu.CompilerParams(vmem_limit_bytes=56 * 2**20, collective_id=1, has_side_effects=True),
         name="attend",
-    )(qkv, halo, augk, augq)
+    )(qkv, augk, augq, out_w, fc_w, proj_w)
 
 
 def attend_back_kernel(
@@ -201,7 +333,7 @@
 
     @pl.when(step == 0)
     def _():
-        fill_keys(heads, qkv_ref, halo_ref, augk_ref, keys, values)
+        plain_fill(heads, qkv_ref, halo_ref, augk_ref, keys, values)
         for h in range(heads):
             for b in range(nkeys // BLK):
                 keys_t[h, :, b * BLK : (b + 1) * BLK] = keys[h, b * BLK : (b + 1) * BLK, :].T
@@ -285,6 +417,7 @@
 def mask_features(segment_ext, docs):
     doc = jnp.arange(docs, dtype=jnp.int32)
     hot = (segment_ext[..., None] == doc).astype(jnp.bfloat16)
+    rows = segment_ext.shape[1]
     outside = (segment_ext < 0).astype(jnp.bfloat16)[..., None]
     pad = HD - docs - 4
     one = jnp.ones(segment_ext.shape + (3,), jnp.bfloat16)
@@ -302,20 +435,445 @@
     return keys, queries
 
 
-norm_eps = 1e-05
-
-
-def standardize(values):
-    centre = values - jnp.mean(values, axis=-1, keepdims=True)
-    spread = jnp.mean(centre * centre, axis=-1, keepdims=True)
-    rate = lax.rsqrt(spread + norm_eps)
-    return centre * rate, rate
-
-
-def norm_grad(direction, z, rate):
-    mean_d = jnp.mean(direction, axis=-1, keepdims=True)
-    mean_dz = jnp.mean(direction * z, axis=-1, keepdims=True)
-    return rate * (direction - mean_d - z * mean_dz)
+def gather_project_kernel(
+    x_ref, small_ref, w_ref, b_ref, all_small_ref, normed_out, qkv_ref,
+    z1, normed, smalls, small_send, small_recv, send_sems, recv_sems, out_sems,
+):
+    group = all_small_ref.shape[0]
+    me = lax.axis_index("fsdp")
+    at = [xor(me, k, group) for k in range(group)]
+    rows = x_ref.shape[0] // 2
+    f32, low = jnp.float32, jnp.bfloat16
+    enter(at[1:])
+
+    def small_copy(k):
+        return pltpu.make_async_remote_copy(
+            src_ref=small_ref, dst_ref=smalls.at[me], send_sem=small_send.at[k], recv_sem=small_recv.at[k],
+            device_id={"fsdp": at[k]}, device_id_type=MESH,
+        )
+
+    for k in range(1, group):
+        small_copy(k).start()
+    smalls[me] = small_ref[...]
+    for s in range(2):
+        z, _ = standardize(x_ref[s * rows : (s + 1) * rows, :].astype(f32))
+        z1[s * rows : (s + 1) * rows, :] = z
+    for k in range(1, group):
+        small_copy(k).wait()
+    all_small_ref[...] = smalls[...]
+    gain = jnp.concatenate([smalls[f, 0:1, :] for f in range(group)], axis=1).astype(f32)
+    offset = jnp.concatenate([smalls[f, 1:2, :] for f in range(group)], axis=1).astype(f32)
+
+    def chunk(p, s):
+        return normed.at[p, s]
+
+    def move(r, s):
+        if r % 2:
+            piece, to = at[r - 1], at[1]
+        elif r == 6:
+            piece, to = (at[2], at[4]) if s == 0 else (at[4], at[2])
+        else:
+            piece, to = me, at[r]
+        return pltpu.make_async_remote_copy(
+            src_ref=chunk(piece, s), dst_ref=chunk(piece, s), send_sem=send_sems.at[r, s], recv_sem=recv_sems.at[r, s],
+            device_id={"fsdp": to}, device_id_type=MESH,
+        )
+
+    def keep(k, s):
+        return pltpu.make_async_copy(chunk(at[k], s), normed_out.at[at[k], s], out_sems.at[k, s])
+
+    def project(k, s):
+        keep(k, s).start()
+        start = pl.multiple_of(at[k] * rows, rows)
+        qkv_ref[s, pl.ds(start, rows), :] = (nn(normed[at[k], s], w_ref[...]) + b_ref[...]).astype(low)
+
+    for s in range(2):
+        normed[me, s] = (z1[s * rows : (s + 1) * rows, :] * gain + offset).astype(low)
+        move(2, s).start()
+        move(4, s).start()
+        move(1, s).start()
+    for s in range(2):
+        project(0, s)
+    for s in range(2):
+        move(1, s).wait_recv()
+        project(1, s)
+    for s in range(2):
+        move(2, s).wait_recv()
+        if s == 0:
+            move(6, 0).start()
+        move(3, s).start()
+        move(4, s).wait_recv()
+        if s == 1:
+            move(6, 1).start()
+        move(5, s).start()
+        project(2, s)
+        project(4, s)
+    for s in range(2):
+        move(3, s).wait_recv()
+        project(3, s)
+        move(5, s).wait_recv()
+        project(5, s)
+    for s in range(2):
+        move(6, s).wait_recv()
+        move(7, s).start()
+        project(6, s)
+    for s in range(2):
+        move(7, s).wait_recv()
+        project(7, s)
+    for s in range(2):
+        for r in range(1, group):
+            move(r, s).wait_send()
+        for k in range(group):
+            keep(k, s).wait()
+
+
+def gather_project(x, small, weight, bias, group):
+    rows, width = x.shape
+    cols = weight.shape[1]
+    half = rows // 2
+    vmem = pl.BlockSpec(memory_space=pltpu.VMEM)
+    low = jnp.bfloat16
+    return pl.pallas_call(
+        gather_project_kernel,
+        in_specs=[vmem] * 4,
+        out_specs=[vmem, pl.BlockSpec(memory_space=pl.ANY), vmem],
+        out_shape=[
+            jax.ShapeDtypeStruct((group,) + small.shape, low),
+            jax.ShapeDtypeStruct((group, 2, half, width), low),
+            jax.ShapeDtypeStruct((2, group * half, cols), low),
+        ],
+        scratch_shapes=[
+            pltpu.VMEM((rows, width), jnp.float32),
+            pltpu.VMEM((group, 2, half, width), low),
+            pltpu.VMEM((group,) + small.shape, low),
+            pltpu.SemaphoreType.DMA((group,)),
+            pltpu.SemaphoreType.DMA((group,)),
+            pltpu.SemaphoreType.DMA((group, 2)),
+            pltpu.SemaphoreType.DMA((group, 2)),
+            pltpu.SemaphoreType.DMA((group, 2)),
+        ],
+        compiler_params=pltpu.CompilerParams(
+            vmem_limit_bytes=48 * 2**20, collective_id=2, has_side_effects=True
+        ),
+        name="gather_project",
+    )(x, small, weight, bias)
+
+
+def gelu_both(v):
+    c = math.sqrt(2.0 / math.pi)
+    square = v * v
+    t = jnp.tanh(v * (c + (c * 0.044715) * square))
+    half = 0.5 * (1.0 + t)
+    slope = half + (0.5 * v) * (1.0 - t * t) * (c + (3.0 * 0.044715 * c) * square)
+    return v * half, slope
+
+
+def column_sums(array):
+    return jnp.sum(array, axis=0, keepdims=True)
+
+
+def feed_forward_kernel(
+    group, x_ref, cot_ref, merged_ref, out_ref, fc_ref, proj_ref, fc_near, proj_near, fcb_ref, vec_ref,
+    layer_ref, gres_ref, gheads_ref, keep_ref, gout_ref, gvec_ref, gfcb_ref,
+    resid, z2, rate, normed, total, gnormed, fc_far, proj_far, given, taken, gmerged, gout_given, gout_taken,
+    far_send, far_recv, pair_send, pair_recv, head_send, head_recv, own_sem, gout_sems,
+):
+    step = pl.program_id(0)
+    last = group - 1
+    me = lax.axis_index("fsdp")
+    at = [xor(me, k, group) for k in range(group)]
+    rows = x_ref.shape[0]
+    block = rows // 2
+    f32, low = jnp.float32, jnp.bfloat16
+    span = merged_ref.shape[1] // group
+
+    def far_copy(a, way):
+        near, far = ((fc_near, fc_far), (proj_near, proj_far))[a]
+        size = near.shape[1] // 2
+        if way == 2:
+            src, dst, to = far.at[1], far.at[0], at[1]
+        else:
+            part = pl.ds(way * size, size)
+            src, dst = near.at[STEP_OF[(2, 4)[way]], part], far.at[1, part]
+            to = at[(4, 2)[way]]
+        return pltpu.make_async_remote_copy(
+            src_ref=src, dst_ref=dst, send_sem=far_send.at[a, way], recv_sem=far_recv.at[a, way],
+            device_id={"fsdp": to}, device_id_type=MESH,
+        )
+
+    def pair_copy(j):
+        return pltpu.make_async_remote_copy(
+            src_ref=given.at[j % 2], dst_ref=taken.at[j], send_sem=pair_send.at[j], recv_sem=pair_recv.at[j],
+            device_id={"fsdp": at[1]}, device_id_type=MESH,
+        )
+
+    def head_copy(k):
+        src = gmerged.at[:, :, pl.ds(k * span, span)]
+        dst = gheads_ref.at[:, pl.ds(pl.multiple_of(me * block, block), block), :]
+        if k == 0:
+            return pltpu.make_async_copy(src, dst, own_sem)
+        return pltpu.make_async_remote_copy(
+            src_ref=src, dst_ref=dst, send_sem=head_send.at[k], recv_sem=head_recv.at[k],
+            device_id={"fsdp": at[k]}, device_id_type=MESH,
+        )
+
+    def gout_copy():
+        return pltpu.make_async_remote_copy(
+            src_ref=gout_given, dst_ref=gout_taken, send_sem=gout_sems.at[0], recv_sem=gout_sems.at[1],
+            device_id={"fsdp": at[1]}, device_id_type=MESH,
+        )
+
+    @pl.when(step == 0)
+    def _():
+        enter(at[1:])
+        for a in range(2):
+            far_copy(a, 0).start()
+            far_copy(a, 1).start()
+        acc = x_ref[...].astype(f32) + vec_ref[0:1, :] + nn(merged_ref[...], out_ref[...])
+        resid[...] = acc
+        z, r = standardize(acc)
+        z2[...] = z
+        rate[...] = jnp.broadcast_to(r, rate.shape)
+        normed[...] = (z * vec_ref[1:2, :] + vec_ref[2:3, :]).astype(low)
+        total[...] = jnp.zeros_like(total)
+        gnormed[...] = jnp.zeros_like(gnormed)
+
+    def work(fc, proj, store):
+        cot = cot_ref[...]
+        hidden = nn(normed[...], fc[...]) + fcb_ref[0]
+        gactive = nt(cot, proj[...])
+        active, slope = gelu_both(hidden)
+        active = active.astype(low)
+        ghidden = gactive * slope
+        gfcb_ref[0] = column_sums(ghidden)
+        ghidden = ghidden.astype(low)
+        total[...] += nn(active, proj[...])
+        gnormed[...] += nt(ghidden, fc[...])
+        gfc = tn(normed[...], ghidden)
+        gproj = tn(active, cot)
+        w, size = gfc.shape[1], gproj.shape[0]
+        store(0, slice(None), gfc)
+        for i in range(gproj.shape[1] // w):
+            store(1, slice(i * size, (i + 1) * size), gproj[:, i * w : (i + 1) * w])
+
+    def give(j):
+        def store(a, part, value):
+            given[j % 2, a, part, :] = value.astype(low)
+
+        return store
+
+    def sum_with(j):
+        def store(a, part, value):
+            keep_ref[0, a, part, :] = (value.astype(low).astype(f32) + taken[j, a, part, :].astype(f32)).astype(low)
+
+        return store
+
+    for i in range(group):
+        slot = SLOT_AT[i]
+        j = slot // 2
+
+        @pl.when(step == i)
+        def _(i=i, slot=slot, j=j):
+            fc, proj = (fc_ref.at[0], proj_ref.at[0]) if i < NEAR else (fc_far.at[i - NEAR], proj_far.at[i - NEAR])
+            if i == NEAR:
+                for a in range(2):
+                    far_copy(a, 2).wait_recv()
+            if slot % 2:
+                if j >= 2:
+                    pair_copy(j - 2).wait_send()
+                work(fc, proj, give(j))
+                pair_copy(j).start()
+            else:
+                pair_copy(j).wait_recv()
+                work(fc, proj, sum_with(j))
+            if i == NEAR - 1:
+                for a in range(2):
+                    far_copy(a, 0).wait_recv()
+                    far_copy(a, 1).wait_recv()
+                    far_copy(a, 2).start()
+
+    @pl.when(step == last)
+    def _():
+        cot32 = cot_ref[...].astype(f32)
+        g, z = gnormed[...], z2[...]
+        gres = cot32 + norm_grad(g * vec_ref[1:2, :], z, rate[:, :1])
+        gres_ref[...] = gres
+        gattn = gres.astype(low)
+        back = nt(gattn, out_ref[...]).astype(low)
+        for s in range(2):
+            gmerged[s] = back[s * block : (s + 1) * block, :]
+        for k in (6, 2, 4, 3, 5, 7, 1, 0):
+            head_copy(k).start()
+        gout = tn(merged_ref[...], gattn)
+        for k in range(1, group, 2):
+            gout_given[k // 2] = gout[k * span : (k + 1) * span, :].astype(low)
+        gout_copy().start()
+        layer_ref[...] = (resid[...] + total[...] + vec_ref[3:4, :]).astype(low)
+        gvec_ref[0:1, :] = column_sums(gattn.astype(f32))
+        gvec_ref[1:2, :] = column_sums(g * z)
+        gvec_ref[2:3, :] = column_sums(g)
+        gvec_ref[3:4, :] = column_sums(cot32)
+        gout_copy().wait_recv()
+        for k in range(0, group, 2):
+            mine = gout[k * span : (k + 1) * span, :].astype(low).astype(f32)
+            gout_ref[k // 2] = (mine + gout_taken[k // 2].astype(f32)).astype(low)
+        for k in range(group):
+            head_copy(k).wait()
+        gout_copy().wait_send()
+        for a in range(2):
+            for way in range(3):
+                far_copy(a, way).wait_send()
+        pair_copy(2).wait_send()
+        pair_copy(3).wait_send()
+
+
+def feed_forward(x, cot, merged, out_all, fc_near, proj_near, fc_bias, vectors):
+    rows, width = x.shape
+    group, part = fc_bias.shape[0], fc_near.shape[2]
+    span = width // group
+    f32, low = jnp.float32, jnp.bfloat16
+    vmem = pl.BlockSpec(memory_space=pltpu.VMEM)
+    hbm = pl.BlockSpec(memory_space=pl.ANY)
+    near = lambda i: jnp.minimum(i, NEAR - 1)
+    kept = lambda i: jnp.where(i == group - 1, 3, jnp.clip(i - 3, 0, 2))
+    return pl.pallas_call(
+        functools.partial(feed_forward_kernel, group),
+        grid=(group,),
+        in_specs=[
+            vmem, vmem, vmem, vmem,
+            pl.BlockSpec((1, width, part), lambda i: (near(i), 0, 0)),
+            pl.BlockSpec((1, part, width), lambda i: (near(i), 0, 0)),
+            hbm, hbm,
+            pl.BlockSpec((1, 1, part), lambda i: (i, 0, 0)),
+            vmem,
+        ],
+        out_specs=[
+            vmem, vmem, hbm,
+            pl.BlockSpec((1, 2, width, part), lambda i: (kept(i), 0, 0, 0)),
+            vmem, vmem,
+            pl.BlockSpec((1, 1, part), lambda i: (i, 0, 0)),
+        ],
+        out_shape=[
+            jax.ShapeDtypeStruct((rows, width), low),
+            jax.ShapeDtypeStruct((rows, width), f32),
+            jax.ShapeDtypeStruct((2, group * rows // 2, span), low),
+            jax.ShapeDtypeStruct((group // 2, 2, width, part), low),
+            jax.ShapeDtypeStruct((group // 2, span, width), low),
+            jax.ShapeDtypeStruct((8, width), f32),
+            jax.ShapeDtypeStruct((group, 1, part), f32),
+        ],
+        scratch_shapes=[
+            pltpu.VMEM((rows, width), f32),
+            pltpu.VMEM((rows, width), f32),
+            pltpu.VMEM((rows, 128), f32),
+            pltpu.VMEM((rows, width), low),
+            pltpu.VMEM((rows, width), f32),
+            pltpu.VMEM((rows, width), f32),
+            pltpu.VMEM((2, width, part), low),
+            pltpu.VMEM((2, part, width), low),
+            pltpu.VMEM((2, 2, width, part), low),
+            pltpu.VMEM((group // 2, 2, width, part), low),
+            pltpu.VMEM((2, rows // 2, width), low),
+            pltpu.VMEM((group // 2, span, width), low),
+            pltpu.VMEM((group // 2, span, width), low),
+            pltpu.SemaphoreType.DMA((2, 3)),
+            pltpu.SemaphoreType.DMA((2, 3)),
+            pltpu.SemaphoreType.DMA((group // 2,)),
+            pltpu.SemaphoreType.DMA((group // 2,)),
+            pltpu.SemaphoreType.DMA((group,)),
+            pltpu.SemaphoreType.DMA((group,)),
+            pltpu.SemaphoreType.DMA,
+            pltpu.SemaphoreType.DMA((2,)),
+        ],
+        compiler_params=pltpu.CompilerParams(vmem_limit_bytes=62 * 2**20, collective_id=3, has_side_effects=True),
+        name="feed_forward",
+    )(x, cot, merged, out_all, fc_near, proj_near, fc_near, proj_near, fc_bias, vectors)
+
+
+def plain_fill(heads, qkv_ref, halo_ref, augk_ref, keys, values):
+    halo_rows = halo_ref.shape[1]
+    rows = qkv_ref.shape[1]
+    ones = jnp.ones((1, HD), jnp.bfloat16)
+    for h in range(heads):
+        c = h * 2 * HD
+        for source, base, size in ((halo_ref, 0, halo_rows), (qkv_ref, halo_rows, rows)):
+            pair = source[0, :, c : c + 2 * HD]
+            keys[h, base : base + size, :] = jnp.concatenate(
+                [pair[:, :HD], augk_ref[0, base : base + size, :]], axis=1
+            )
+            values[h, base : base + size, :] = jnp.concatenate(
+                [pair[:, HD:], jnp.broadcast_to(ones, (size, HD))], axis=1
+            )
+
+
+def plain_attend_kernel(heads, qkv_ref, halo_ref, augk_ref, augq_ref, out_ref, q2_ref, keys, values, values_t):
+    step = pl.program_id(1)
+    nkeys = keys.shape[1]
+
+    @pl.when(step == 0)
+    def _():
+        plain_fill(heads, qkv_ref, halo_ref, augk_ref, keys, values)
+        for h in range(heads):
+            for b in range(nkeys // BLK):
+                values_t[h, :, b * BLK : (b + 1) * BLK] = values[h, b * BLK : (b + 1) * BLK, :].T
+
+    mask = edge_mask()
+    tiles = WINDOW // BLK + 1
+    start = pl.multiple_of(step * BLK, BLK)
+    lane = lax.broadcasted_iota(jnp.int32, (BLK, 2 * HD), 1)
+    lse_lane = augq_ref.shape[2] + HD - 3
+    for h in range(heads):
+        qc = heads * 2 * HD + h * HD
+        q = jnp.concatenate([qkv_ref[0, pl.ds(start, BLK), qc : qc + HD] * 0.125, augq_ref[0]], axis=1)
+        scores = [nt(keys[h, pl.ds(start + b * BLK, BLK), :], q) for b in range(tiles)]
+        scores = merge_edges(mask, scores)
+        peak = functools.reduce(jnp.maximum, scores)
+        peak = jnp.max(peak, axis=0, keepdims=True)
+        weights = spread_edges(mask, [jnp.exp(s - peak).astype(jnp.bfloat16) for s in scores])
+        total = sum(
+            nn(values_t[h, :, pl.ds(pl.multiple_of(start + b * BLK, BLK), BLK)], w) for b, w in enumerate(weights)
+        )
+        sub = lax.broadcasted_iota(jnp.int32, total.shape, 0)
+        total = jnp.where(sub == HD + 1, peak, total).T
+        norm = total[:, HD : HD + 1]
+        out_ref[0, :, h * HD : (h + 1) * HD] = (total[:, :HD] / norm).astype(out_ref.dtype)
+        lse = total[:, HD + 1 : HD + 2] + jnp.log(norm)
+        hi, mid, low = split3(-lse)
+        q2 = q.astype(jnp.float32)
+        q2 = jnp.where(lane == lse_lane, hi, q2)
+        q2 = jnp.where(lane == lse_lane + 1, mid, q2)
+        q2 = jnp.where(lane == lse_lane + 2, low, q2)
+        q2_ref[0, h] = q2.astype(jnp.bfloat16)
+
+
+def plain_attend(qkv, halo, augk, augq, heads):
+    seqs, rows, cols = qkv.shape
+    ext = augk.shape[1]
+    return pl.pallas_call(
+        functools.partial(plain_attend_kernel, heads),
+        grid=(seqs, rows // BLK),
+        in_specs=[
+            pl.BlockSpec((1, rows, cols), lambda s, i: (s, 0, 0)),
+            pl.BlockSpec((1, WINDOW, heads * 2 * HD), lambda s, i: (s, 0, 0)),
+            pl.BlockSpec((1, ext, HD), lambda s, i: (s, 0, 0)),
+            pl.BlockSpec((1, BLK, HD), lambda s, i: (s, i, 0)),
+        ],
+        out_specs=[
+            pl.BlockSpec((1, BLK, heads * HD), lambda s, i: (s, i, 0)),
+            pl.BlockSpec((1, heads, BLK, 2 * HD), lambda s, i: (s, 0, i, 0)),
+        ],
+        out_shape=[
+            jax.ShapeDtypeStruct((seqs, rows, heads * HD), jnp.bfloat16),
+            jax.ShapeDtypeStruct((seqs, heads, rows, 2 * HD), jnp.bfloat16),
+        ],
+        scratch_shapes=[
+            pltpu.VMEM((heads, ext, 2 * HD), jnp.bfloat16),
+            pltpu.VMEM((heads, ext, 2 * HD), jnp.bfloat16),
+            pltpu.VMEM((heads, 2 * HD, ext), jnp.bfloat16),
+        ],
+        compiler_params=pltpu.CompilerParams(vmem_limit_bytes=48 * 2**20),
+        name="plain_attend",
+    )(qkv, halo, augk, augq)
 
 
 def from_behind(block, axis, distance):
@@ -343,7 +901,7 @@
     return jnp.einsum(subscripts, a, b, preferred_element_type=jnp.float32)
 
 
-def body(
+def general_body(
     inputs, cotangent, segment_ids, norm1_gain, norm1_bias, qkv_weight, qv_bias, out_weight, out_bias,
     norm2_gain, norm2_bias, fc_weight, fc_bias, proj_weight, proj_bias,
 ):
@@ -381,9 +939,8 @@
     packed_bias = pack_columns(head_bias, heads)
     qkv = (dot("sre,ef->srf", normed1, packed_weight) + packed_bias).astype(jnp.bfloat16)
     halo = from_behind(qkv[:, part_rows - WINDOW :, : heads * 2 * HD], "seq", 1)
-    head_out, q2, merged = attend(qkv, halo, augk, augq, heads, group)
-    me = lax.axis_index("fsdp")
-    merged = jnp.stack([lax.dynamic_index_in_dim(merged, xor(me, k, group), 0, False) for k in range(group)], axis=2).reshape(seqs, local_rows, width)
+    head_out, q2 = plain_attend(qkv, halo, augk, augq, heads)
+    merged = lax.all_to_all(head_out, "fsdp", split_axis=1, concat_axis=2, tiled=True)
     resid = x + dot("sre,ef->srf", merged, out_all) + out_off
     z2, rate2 = standardize(resid)
     normed2 = (z2 * gain2 + offset2).astype(jnp.bfloat16)
@@ -448,11 +1005,100 @@
     )
 
 
+def cube_body(
+    inputs, cotangent, segment_ids, norm1_gain, norm1_bias, qkv_weight, qv_bias, out_weight, out_bias,
+    norm2_gain, norm2_bias, fc_weight, fc_bias, proj_weight, proj_bias,
+):
+    group = lax.axis_size("fsdp")
+    seqs, local_rows, width = inputs.shape
+    part_rows = local_rows * group
+    heads = qkv_weight.shape[1] // (3 * HD)
+    docs = segment_ids.shape[1] // (2 * WINDOW)
+    seq_index = lax.axis_index("seq")
+    me = lax.axis_index("fsdp")
+    shard = norm1_gain.shape[0]
+    f32, low = jnp.float32, jnp.bfloat16
+
+    small = jnp.concatenate([norm1_gain, norm1_bias, out_bias, norm2_gain, norm2_bias, proj_bias, fc_bias])
+    small = jnp.pad(small, (0, 16 * shard - small.shape[0])).reshape(16, shard)
+    padded_ids = jnp.concatenate([jnp.full((seqs, WINDOW), -1, jnp.int32), segment_ids], axis=1)
+    segment_ext = lax.dynamic_slice_in_dim(padded_ids, seq_index * part_rows, WINDOW + part_rows, 1)
+    augk, augq = mask_features(segment_ext, docs)
+    packed_weight = pack_columns(qkv_weight, heads)
+    head_bias = qv_bias.astype(f32)
+    head_bias = jnp.concatenate(
+        [head_bias[:, :HD], jnp.zeros((heads, HD), f32), head_bias[:, HD:]], axis=1
+    ).reshape(-1)
+    packed_bias = pack_columns(head_bias, heads)
+
+    x = inputs.reshape(seqs * local_rows, width)
+    cot = cotangent.reshape(seqs * local_rows, width)
+    all_small, normed1, qkv = gather_project(x, small, packed_weight, packed_bias[None], group)
+    head_out, q2, halo, merged, out_all, fc_near, proj_near = attend(
+        qkv, augk, augq, out_weight, fc_weight, proj_weight, heads, group
+    )
+    full = lambda i: all_small[:, i].reshape(-1).astype(f32)
+    gain1 = full(0)
+    vectors = jnp.stack([full(2), full(3), full(4), full(5)] + [jnp.zeros((width,), f32)] * 4)
+    slots = jnp.stack([xor(me, r, group) for r in SLOT_AT])
+    fc_off = jnp.take(all_small[:, 6:10].reshape(group, -1), slots, axis=0).astype(f32)[:, None]
+    layer_output, g_resid, g_heads, kept, out_kept, gvec, gfcb = feed_forward(
+        x, cot, merged.reshape(x.shape), out_all.reshape(width, width), fc_near, proj_near, fc_off, vectors
+    )
+    dq, dkv, dhalo = attend_back(qkv, halo, augk, q2, head_out, g_heads, heads)
+
+    def swap(v, bit):
+        return lax.ppermute(v, "fsdp", [(i, i ^ bit) for i in range(group)])
+
+    def add(u, v):
+        return (u.astype(f32) + v.astype(f32)).astype(low)
+
+    def scatter(first, second, s2, s4, s0, s6):
+        r2, r6 = swap(s2, first), swap(s6, first)
+        return add(add(s0, r2), swap(add(s4, r6), second))
+
+    f2, f4, f0, f6 = (kept[i, 0] for i in range(4))
+    p2, p4, p0, p6 = (kept[i, 1] for i in range(4))
+    fc_grad = scatter(2, 4, f2, f4, f0, f6)
+    proj_grad = scatter(4, 2, p4, p2, p0, p6)
+    out_grad = scatter(2, 4, out_kept[1], out_kept[2], out_kept[0], out_kept[3])
+    w = proj_grad.shape[1]
+    proj_grad = jnp.concatenate([proj_grad[: proj_grad.shape[0] // 2], proj_grad[proj_grad.shape[0] // 2 :]], axis=1)
+    fc_grad, proj_grad, out_grad = lax.psum((fc_grad, proj_grad, out_grad), "seq")
+
+    edge = from_behind(dhalo, "seq", -1)
+    edge = jnp.pad(edge.astype(f32), ((0, 0), (part_rows - WINDOW, 0), (0, 0)))
+    g_qkv = jnp.concatenate([(dkv + edge).astype(low), dq], axis=-1)
+    qkv_colsum = jnp.sum(g_qkv, axis=(0, 1), dtype=f32)
+    g_norm1 = dot("srf,ef->sre", g_qkv, packed_weight).astype(low)
+    g_norm1 = lax.psum_scatter(g_norm1, "fsdp", scatter_dimension=1, tiled=True).astype(f32)
+    qkv_grad = dot("fsre,sfrc->ec", normed1, g_qkv.reshape(seqs, group, local_rows, -1))
+    z1, rate1 = standardize(inputs.astype(f32))
+    gain1_part = jnp.sum(g_norm1 * z1, axis=(0, 1))
+    offset1_part = jnp.sum(g_norm1, axis=(0, 1))
+    g_resid = g_resid.reshape(inputs.shape)
+    input_grad = (g_resid + norm_grad(g_norm1 * gain1, z1, rate1)).astype(low)
+    qkv_grad = lax.psum(qkv_grad.astype(low), "seq").astype(f32)
+    qkv_grad = unpack_columns(qkv_grad, heads)
+    col = unpack_columns(qkv_colsum, heads).reshape(heads, 3 * HD)
+    col = lax.psum(jnp.concatenate([col[:, :HD], col[:, 2 * HD :]], axis=1), "seq")
+    back = jnp.zeros((group, fc_bias.shape[0]), f32).at[slots].set(gfcb[:, 0])
+    vecs = jnp.concatenate(
+        [v.reshape(group, -1) for v in (gain1_part, offset1_part, gvec[0], gvec[1], gvec[2], gvec[3], back)], axis=1
+    )
+    vecs = lax.psum(lax.psum_scatter(vecs, "fsdp"), "seq")
+    parts = [vecs[i * shard : (i + 1) * shard] for i in range(6)] + [vecs[6 * shard :]]
+    return (
+        layer_output.reshape(inputs.shape), input_grad, parts[0], parts[1], qkv_grad, col, out_grad.astype(f32),
+        parts[2], parts[3], parts[4], fc_grad.astype(f32), parts[6], proj_grad.astype(f32), parts[5],
+    )
+
+
 def solution(mesh):
     tokens = P(None, ("seq", "fsdp"), None)
     rows, cols, vec = P("fsdp", None), P(None, "fsdp"), P("fsdp")
     return jax.shard_map(
-        body,
+        cube_body if mesh.shape["fsdp"] == 8 and mesh.shape["seq"] == 4 else general_body,
         mesh=mesh,
         in_specs=(tokens, tokens, P(), vec, vec, cols, rows, rows, vec, vec, vec, cols, vec, rows, vec),
         out_specs=(tokens, tokens, vec, vec, cols, rows, rows, vec, vec, vec, cols, vec, rows, vec),

time: 674 us -> 575 us (0.85)
  Pallas kernels: 83.7 us -> 239 us
  waiting for transfers between devices: 336 us -> 194 us
  matrix products: 99.7 us -> 13.4 us
  blocking collectives: 69.8 us -> 35.2 us
  local copies, waits for them, and re-layouts: 32.1 us -> 22.3 us
  other arithmetic: 26.1 us -> 34.5 us
    pallas_call x0 -> x2, Pallas kernels: none -> 118 us  [the longest x1 71.6 us: feed_forward(): pl.pallas_call(functools.partial(feed_forward_kernel, group), grid=(group...]
    reduce_scatter x4 -> x1, waiting for transfers between devices: 111 us -> 0.01 us  [cube_body(): lax.psum_scatter(g_norm1, 'fsdp', scatter_dimension=1, tiled=True)]
    all_gather x4 -> x0, waiting for transfers between devices: 102 us -> none  [the longest x1 48.1 us: body(): normed1 = lax.all_gather(normed1, 'fsdp', axis=1, tiled=True)]
    dot_general x12 -> x2, matrix products: 99.7 us -> 13.4 us  [dot(): return jnp.einsum(subscripts, a, b, preferred_element_type=jnp.float32)]
    ppermute x0 -> x9, waiting for transfers between devices: none -> 83 us  [swap(): return lax.ppermute(v, 'fsdp', [(i, i ^ bit) for i in range(group)])]
    ppermute x2 -> x1, waiting for transfers between devices: 41.3 us -> 0.01 us  [from_behind(): return lax.ppermute(block, axis, route)]
    pallas_call x1, Pallas kernels: 42.7 us -> 80.2 us  [attend(): pl.pallas_call(functools.partial(attend_kernel, heads, group), grid=(seqs...]
    psum x1, waiting for transfers between devices: 80.1 us -> 111 us  [cube_body(): qkv_grad = lax.psum(qkv_grad.astype(low), 'seq').astype(f32)]
  transfers between devices with their start and end apart: 11 -> 12, of which waited for: 8 -> 4; matrix products, arithmetic and copies ran while one was open for 16% -> 6% of each run, Pallas kernels for 13% -> 7%
where the time goes in v3:
time: 575 us; the launch traced here: 565 us
  Pallas kernels  239 us (42%)
  waiting for transfers between devices  194 us (34%)
  blocking collectives  35.2 us (6%)
  other arithmetic  34.5 us (6%)
  local copies, waits for them, and re-layouts  22.3 us (4%)
  between operations  16.3 us (3%)
  matrix products  13.4 us (2%)
  starting transfers between devices  10.3 us (2%)
    psum x1, waiting for transfers between devices, cube_body(): qkv_grad = lax.psum(qkv_grad.astype(low), 'seq').astype(f32)  111 us
    ppermute x9, waiting for transfers between devices, swap(): return lax.ppermute(v, 'fsdp', [(i, i ^ bit) for i in range(group)])  83 us
    pallas_call x1, Pallas kernels, attend(): pl.pallas_call(functools.partial(attend_kernel, heads, group), grid=(seqs...  80.2 us
    pallas_call x1, Pallas kernels, feed_forward(): pl.pallas_call(functools.partial(feed_forward_kernel, group), grid=(group...  71.6 us
    pallas_call x1, Pallas kernels, gather_project(): pl.pallas_call(gather_project_kernel, in_specs=[vmem] * 4, out_specs=[vme...  46.7 us
    pallas_call x1, Pallas kernels, attend_back(): pl.pallas_call(functools.partial(attend_back_kernel, heads), grid=(seqs,...  40.5 us
    unnamed x1, blocking collectives  24.4 us
    dot_general x2, matrix products, dot(): return jnp.einsum(subscripts, a, b, preferred_element_type=jnp.float32)  13.4 us
  transfers between devices with their start and end apart: 12, of which 4 were waited for; matrix products, arithmetic and copies ran while one was open for 6% of the time, Pallas kernels for 7%

profile of v3, /device:TPU:0, one launch (start us, length us, event | category | flops | bytes accessed | tf_op | source)
XLA Modules:
  0.0 565.3 jit_solution(3651791460284360443)
XLA Ops:
  12.1 46.7 %gather_project.1 = (bf16[8,16,128]{2,1,0:T(8,128)(2,1)S(1)}, bf16[8,2,256,1024]{3,2,1,0:T(8,128)(2,1)}, bf16[2,2048,384]{2,1,0:T(8,128)(2,1)S(1)}) custom-call(bf16[512,1024]{1,0:T(8,128)(2,1)S(1)} %bitcast.110, bf16[16,128]{1,0:T(8,128)(2,1)S(1)} %pad_bitcast_fusion.small_ref, bf16[1024,384]{1,0:T(8,128)(2,1)S(1)} %pad_maximum_fusion.3.w_ref, ...), custom_call_target="tpu_custom_call" | custom-call | tf_op jit(solution)/shard_map/gather_project/pallas_call | solution.py:536
  58.8 1.6 copy-done.2
  61.7 2.3 fusion.2
  65.4 2.3 fusion.22
  69.2 2.5 maximum_maximum_fusion.1.augq_ref
  71.7 2.2 maximum_maximum_fusion.augk_ref
  74.6 80.2 %attend.1 = (bf16[2,2048,128]{2,1,0:T(8,128)(2,1)}, bf16[2,2,2048,128]{3,2,1,0:T(8,128)(2,1)}, bf16[2,1024,256]{2,1,0:T(8,128)(2,1)}, bf16[2,256,1024]{2,1,0:T(8...) custom-call(bf16[2,2048,384]{2,1,0:T(8,128)(2,1)} %copy-done.2, ...), custom_call_target="tpu_custom_call" | custom-call | tf_op jit(solution)/shard_map/attend/pallas_call | solution.py:296
  154.8 71.6 %feed_forward.1 = (bf16[512,1024]{1,0:T(8,128)(2,1)}, f32[512,1024]{1,0:T(8,128)}, bf16[2,2048,128]{2,1,0:T(8,128)(2,1)}, bf16[4,2,1024,512]{3,2,1,0:T(8,128)(2,...) custom-call(bf16[512,1024]{1,0:T(8,128)(2,1)} %bitcast.109, ...), custom_call_target="tpu_custom_call" | custom-call | tf_op jit(solution)/shard_map/feed_forward/pallas_call | solution.py:739
  226.5 4.0 slice_bitcast_fusion.1
  232.7 40.5 %attend_back.1 = (bf16[2,2048,128]{2,1,0:T(8,128)(2,1)}, f32[2,2048,256]{2,1,0:T(8,128)}, bf16[2,1024,256]{2,1,0:T(8,128)(2,1)}) custom-call(bf16[2,2048,384]{2,1,0:T(8,128)(2,1)} %copy-done.2, bf16[2,1024,256]{2,1,0:T(8,128)(2,1)} %get-tuple-element.42.halo_ref, bf16[2,3072,64]{2,1,0:T(8,128)(2,1)} %maximum_maximum_fusion.augk_ref, ...), custom_call_target="tpu_custom_call" | custom-call | tf_op jit(solution)/shard_map/attend_back/pallas_call | solution.py:384
  280.3 24.9 %collective-permute-done.1 = bf16[128,1024]{1,0:T(8,128)(2,1)S(1)} collective-permute-done((bf16[128,1024]{1,0:T(8,128)(2,1)S(1)}, bf16[128,1024]{1,0:T(8,128)(2,1)S(1)}, u32[]{:S(2)}, u32[]{:S(2)}) %collective-permute-start.1) | collective-permute-done | bytes 262176 | tf_op jit(solution)/shard_map/ppermute | solution.py:1051
  309.6 42.2 %collective-permute-done.9 = bf16[1024,512]{1,0:T(8,128)(2,1)S(1)} collective-permute-done((bf16[1024,512]{1,0:T(8,128)(2,1)S(1)}, bf16[1024,512]{1,0:T(8,128)(2,1)S(1)}, u32[]{:S(2)}, u32[]{:S(2)}) %collective-permute-start.9) | collective-permute-done | bytes 1048608 | tf_op jit(solution)/shard_map/ppermute | solution.py:1051
  351.7 2.3 add_convert_fusion.1
  354.7 5.4 bitcast_convert_fusion
  361.2 15.9 %collective-permute-done.6 = bf16[1024,512]{1,0:T(8,128)(2,1)S(1)} collective-permute-done((bf16[1024,512]{1,0:T(8,128)(2,1)S(1)}, bf16[1024,512]{1,0:T(8,128)(2,1)S(1)}, u32[]{:S(2)}, u32[]{:S(2)}) %collective-permute-start.6) | collective-permute-done | bytes 1048608 | tf_op jit(solution)/shard_map/ppermute | solution.py:1051
  377.1 2.6 add_convert_fusion.2
  379.8 8.0 %convolution_convert_fusion = bf16[2,2048,1024]{2,1,0:T(8,128)(2,1)} fusion(bf16[1024,128]{1,0:T(8,128)(2,1)S(1)} %copy.43, bf16[1024,256]{1,0:T(8,128)(2,1)} %copy-done.8, bf16[2,2048,128]{2,1,0:T(8,128)(2,1)S(1)} %copy-done.5, bf16[2,2048,256]{2,1,0:T(8,128)(2,1)S(1)} %add_convert_fusion), kind=kOutput, calls=%fused_computation.3 | convolution fusion | flops 3233284096 | bytes 12320768 | tf_op jit(solution)/shard_map/srf,ef->sre/dot_general | solution.py:901
  391.4 111.1 %all-reduce.9.cloned.1.call-done = (bf16[1024,384]{1,0:T(8,128)(2,1)}, bf16[128,1024]{1,0:T(8,128)(2,1)}, bf16[1024,512]{1,0:T(8,128)(2,1)}, bf16[512,1024]{1,0:T(8,128)(2,1)}) async-done(((bf16[1024,384]{1,0:T(8,128)(2,1)}, bf16[128,1024]{1,0:T(8,128)(2,1)}, bf16[1024,512]{1,0:T(8,128)(2,1)}, bf16[512,1024]{1,0:T(8,128)(2,1)}), (bf16[1024,384]{1,0:T(8,128)(2,1)}, bf16[128,1024]{1,0:T(8,128)(2,1)}, ...) | async-done | bytes 3145744 | tf_op jit(solution)/shard_map/psum | solution.py:1081
  506.7 1.6 copy.50
  508.4 2.9 convert_element_type.263
  513.7 2.4 fusion.15
  516.2 24.4 %all-reduce.4 = f32[8,1280]{1,0:T(8,128)S(1)} all-reduce(f32[8,1280]{1,0:T(8,128)S(1)} %constant_dynamic-update-slice_fusion), channel_id=3, replica_groups=mesh['seq'=4,'fsdp'=8] {'fsdp'}, use_global_device_ids=true, to_apply=%region_8.9.clone | all-reduce | flops 10240 | bytes 81920
  541.3 10.8 %all-reduce.5 = (f32[1280]{0:T(1024)S(1)}, f32[2,128]{1,0:T(2,128)}) all-reduce(f32[1280]{0:T(1024)S(1)} %dynamic-slice_reduce_fusion, f32[2,128]{1,0:T(2,128)S(1)} %pad_maximum_fusion.5), channel_id=1, replica_groups=mesh['seq'=4,'fsdp'=8] {'seq'}, use_global_device_ids=true, to_apply=%region_9.10 | all-reduce | flops 1536 | bytes 12288 | tf_op jit(solution)/shard_map/psum | solution.py:1089
  553.2 3.4 fusion.12
  (158 shorter events, 36.7 us)
Async XLA Ops:
  8.0 494.5 %all-reduce.9.cloned.1.call-start = ((), (), s32[]{:S(2)}) async-start(), calls=%async_computation.2 | async-start | bytes 6291456 | tf_op jit(solution)/shard_map/psum | solution.py:1081
  8.1 2.9 copy-start.21
  8.1 3.2 copy-start.22
  8.2 3.4 copy-start.23
  8.2 3.6 copy-start.17
  9.9 50.6 %copy-start.8 = (bf16[1024,256]{1,0:T(8,128)(2,1)}, bf16[1024,256]{1,0:T(8,128)(2,1)S(1)}, u32[]{:S(2)}) copy-start(bf16[1024,256]{1,0:T(8,128)(2,1)S(1)} %copy.53) | copy-start | bytes 1572868
  9.9 50.5 %copy-start.13 = (s32[2,8192]{1,0:T(2,128)S(1)}, s32[2,8192]{1,0:T(2,128)}, u32[]{:S(2)}) copy-start(s32[2,8192]{1,0:T(2,128)} %param.17) | copy-start | bytes 196612
  226.5 4.6 copy-start.11
  230.5 46.7 %collective-permute-start.8 = (bf16[1024,512]{1,0:T(8,128)(2,1)S(1)}, bf16[1024,512]{1,0:T(8,128)(2,1)S(1)}, u32[]{:S(2)}, u32[]{:S(2)}) collective-permute-start(bf16[1024,512]{1,0:T(8,128)(2,1)S(1)} %get-tuple-element.97), channel_id=1, source_target_pairs={{0,4},{1,5},{2,6},{3,7},{4,0},{5,1},{6,2},{7,3},{8,12},{9,13},{10,... | collective-permute-start | bytes 3145736 | tf_op jit(solution)/shard_map/ppermute | solution.py:1051
  231.1 45.4 %collective-permute-start.2 = (bf16[128,1024]{1,0:T(8,128)(2,1)S(1)}, bf16[128,1024]{1,0:T(8,128)(2,1)S(1)}, u32[]{:S(2)}, u32[]{:S(2)}) collective-permute-start(bf16[128,1024]{1,0:T(8,128)(2,1)S(1)} %get-tuple-element.103), channel_id=1, source_target_pairs={{0,2},{1,3},{2,0},{3,1},{4,6},{5,7},{6,4},{7,5},{8,10},{9,11},{10,... | collective-permute-start | bytes 786440 | tf_op jit(solution)/shard_map/ppermute | solution.py:1051
  273.2 34.8 %collective-permute-start = (bf16[2,1024,256]{2,1,0:T(8,128)(2,1)}, bf16[2,1024,256]{2,1,0:T(8,128)(2,1)S(1)}, u32[]{:S(2)}, u32[]{:S(2)}) collective-permute-start(bf16[2,1024,256]{2,1,0:T(8,128)(2,1)} %get-tuple-element.47), channel_id=1, source_target_pairs={{8,0},{16,8},{24,16},{9,1},{17,9},{25,17},{10,2},{18,10},{26,18},{... | collective-permute-start | bytes 3145736 | tf_op jit(solution)/shard_map/ppermute | solution.py:882
  274.5 35.1 %collective-permute-start.5 = (bf16[1024,512]{1,0:T(8,128)(2,1)}, bf16[1024,512]{1,0:T(8,128)(2,1)S(1)}, u32[]{:S(2)}, u32[]{:S(2)}) collective-permute-start(bf16[1024,512]{1,0:T(8,128)(2,1)} %get-tuple-element.98), channel_id=1, source_target_pairs={{0,2},{1,3},{2,0},{3,1},{4,6},{5,7},{6,4},{7,5},{8,10},{9,11},{10,... | collective-permute-start | bytes 3145736 | tf_op jit(solution)/shard_map/ppermute | solution.py:1051
  275.1 34.5 %collective-permute-start.7 = (bf16[1024,512]{1,0:T(8,128)(2,1)}, bf16[1024,512]{1,0:T(8,128)(2,1)S(1)}, u32[]{:S(2)}, u32[]{:S(2)}) collective-permute-start(bf16[1024,512]{1,0:T(8,128)(2,1)} %get-tuple-element.96), channel_id=1, source_target_pairs={{0,4},{1,5},{2,6},{3,7},{4,0},{5,1},{6,2},{7,3},{8,12},{9,13},{10,... | collective-permute-start | bytes 3145736 | tf_op jit(solution)/shard_map/ppermute | solution.py:1051
  276.5 28.6 %collective-permute-start.1 = (bf16[128,1024]{1,0:T(8,128)(2,1)S(1)}, bf16[128,1024]{1,0:T(8,128)(2,1)S(1)}, u32[]{:S(2)}, u32[]{:S(2)}) collective-permute-start(bf16[128,1024]{1,0:T(8,128)(2,1)S(1)} %get-tuple-element.102), channel_id=1, source_target_pairs={{0,2},{1,3},{2,0},{3,1},{4,6},{5,7},{6,4},{7,5},{8,10},{9,11},{10,... | collective-permute-start | bytes 786440 | tf_op jit(solution)/shard_map/ppermute | solution.py:1051
  277.2 30.8 %copy-start.3 = (f32[2,2048,256]{2,1,0:T(8,128)S(1)}, f32[2,2048,256]{2,1,0:T(8,128)}, u32[]{:S(2)}) copy-start(f32[2,2048,256]{2,1,0:T(8,128)} %get-tuple-element.46) | copy-start | bytes 12582916
  277.2 28.5 %collective-permute-start.3 = (bf16[128,1024]{1,0:T(8,128)(2,1)S(1)}, bf16[128,1024]{1,0:T(8,128)(2,1)S(1)}, u32[]{:S(2)}, u32[]{:S(2)}) collective-permute-start(bf16[128,1024]{1,0:T(8,128)(2,1)S(1)} %fusion.24), channel_id=1, source_target_pairs={{0,4},{1,5},{2,6},{3,7},{4,0},{5,1},{6,2},{7,3},{8,12},{9,13},{10,... | collective-permute-start | bytes 786440 | tf_op jit(solution)/shard_map/ppermute | solution.py:1051
  305.2 56.1 %collective-permute-start.4 = (bf16[1024,512]{1,0:T(8,128)(2,1)}, bf16[1024,512]{1,0:T(8,128)(2,1)S(1)}, u32[]{:S(2)}, u32[]{:S(2)}) collective-permute-start(bf16[1024,512]{1,0:T(8,128)(2,1)} %get-tuple-element.99), channel_id=1, source_target_pairs={{0,2},{1,3},{2,0},{3,1},{4,6},{5,7},{6,4},{7,5},{8,10},{9,11},{10,... | collective-permute-start | bytes 3145736 | tf_op jit(solution)/shard_map/ppermute | solution.py:1051
  305.7 46.0 %collective-permute-start.9 = (bf16[1024,512]{1,0:T(8,128)(2,1)S(1)}, bf16[1024,512]{1,0:T(8,128)(2,1)S(1)}, u32[]{:S(2)}, u32[]{:S(2)}) collective-permute-start(bf16[1024,512]{1,0:T(8,128)(2,1)S(1)} %fusion.16), channel_id=1, source_target_pairs={{0,2},{1,3},{2,0},{3,1},{4,6},{5,7},{6,4},{7,5},{8,10},{9,11},{10,... | collective-permute-start | bytes 3145736 | tf_op jit(solution)/shard_map/ppermute | solution.py:1051
  308.0 46.7 %slice-start = ((s8[8388608]{0:T(1024)(128)(4,1)}), s8[4194304]{0:T(1024)(128)(4,1)S(1)}, s32[]{:S(2)}) async-start(s8[8388608]{0:T(1024)(128)(4,1)} %bitcast.132), calls=%async_computation.3 | async-start | bytes 8388608
  309.2 45.4 %slice-start.1 = ((s8[8388608]{0:T(1024)(128)(4,1)}), s8[4194304]{0:T(1024)(128)(4,1)S(1)}, s32[]{:S(2)}) async-start(s8[8388608]{0:T(1024)(128)(4,1)} %bitcast.132), calls=%async_computation.4 | async-start | bytes 8388608
  354.1 23.1 %collective-permute-start.6 = (bf16[1024,512]{1,0:T(8,128)(2,1)S(1)}, bf16[1024,512]{1,0:T(8,128)(2,1)S(1)}, u32[]{:S(2)}, u32[]{:S(2)}) collective-permute-start(bf16[1024,512]{1,0:T(8,128)(2,1)S(1)} %get-tuple-element.95), channel_id=1, source_target_pairs={{0,4},{1,5},{2,6},{3,7},{4,0},{5,1},{6,2},{7,3},{8,12},{9,13},{10,... | collective-permute-start | bytes 3145736 | tf_op jit(solution)/shard_map/ppermute | solution.py:1051
  379.8 133.9 %reduce-scatter.2.cloned.1.call-start = ((), (), s32[]{:S(2)}) async-start(), calls=%async_computation.1 | async-start | bytes 9437184 | tf_op jit(solution)/shard_map/reduce_scatter | solution.py:1074
  513.7 39.5 %copy-start.4 = (bf16[2,256,1024]{2,1,0:T(8,128)(2,1)S(1)}, bf16[2,256,1024]{2,1,0:T(8,128)(2,1)}, u32[]{:S(2)}) copy-start(bf16[2,256,1024]{2,1,0:T(8,128)(2,1)} %reduce-scatter.2.cloned.1.call-done) | copy-start | bytes 3145732
  553.2 3.4 copy-start.10
  (15 other events, 28.5 us)
Sparse Core Ops, SparseCore 0:
  379.9 122.6 all-reduce.8
Sparse Core Ops, SparseCore 1:
  388.0 71.6 reduce-scatter.1
